TPU v7x, 128 devices: a whole 4x4x4 slice. The times are simulated.
128 devices in a mesh: row: 16 (over z, y), col: 8 (over x, core).
Axes of the slice: x: 4, y: 4, z: 4, core: 2. Of those that a mesh axis runs over, the one named last changes fastest.
Arguments:
- child_fronts: float32 [128, 2048, 2048], P(('row', 'col')), may hold values from -3 to 20, as said below
- child_tiles: int32 [128, 12], P(('row', 'col')), may hold values from 0 to 63, as said below
- parent_front: float32 [8192, 8192], P('row', 'col'), may hold values from -5 to 20, as said below
Outputs:
- child_factors: float32 [128, 2048, 512], P(('row', 'col'))
- parent_result: float32 [8192, 8192], P('row', 'col')
Inputs may be any that keep to these rules, and one draw needn't show every extreme that they name: `child_tiles`: each row holds strictly increasing parent tile indices, no two of them in the same group of 4 consecutive tiles. `child_fronts`: each child front is symmetric positive definite. `parent_front`: symmetric positive definite.
All inputs are finite; a program needn't handle non-finite values.
Results may differ from a plain program's by a relative error of at most 0.0003.
Values sent between devices are 32-bit elements; how exact they have to be, the bound alone decides.
No kernel may reach another device: no remote copies, remote signals or barrier semaphores. Data moves between devices by JAX's collectives and lax.ppermute only.
A program may use at most 192 MiB of HBM per device.

v0:
```python
import jax
import jax.numpy as jnp
from jax import lax
from jax.sharding import PartitionSpec as P

PANEL = 512
TILE = 128
CP = 512
PANELS = 2
TPB = 4
NB = 16
CT = 12


PRECISE = lax.Precision.HIGHEST


def from_root(value, axis, source):
    kept = jnp.where(lax.axis_index(axis) == source, value, 0).astype(value.dtype)
    return lax.psum(kept, axis)


def product(left_side, right_side):
    return lax.dot_general(
        left_side,
        right_side,
        (((1,), (1,)), ((), ())),
        precision=PRECISE,
        preferred_element_type=jnp.float32,
    )


def right_solve(factor, right_block):
    return jax.scipy.linalg.solve_triangular(factor, right_block.T, lower=True).T


def eliminate_child(matrix):
    corner = jnp.linalg.cholesky(matrix[:CP, :CP])
    below_rows = right_solve(corner, matrix[CP:, :CP])
    update = matrix[CP:, CP:] - product(below_rows, below_rows)
    return (jnp.concatenate([corner, below_rows], axis=0), update)


def keep_blocks(panel_block, block_ids, pivot_step, corner):
    block_count = block_ids.shape[0]
    stacked = panel_block.reshape(block_count, PANEL, PANEL)
    chosen = jnp.where((block_ids > pivot_step)[:, None, None], stacked, 0.0)
    chosen = jnp.where((block_ids == pivot_step)[:, None, None], corner[None], chosen)
    return chosen.reshape(block_count * PANEL, PANEL)


def locate(everyone, targets):
    matches = (everyone // TPB)[:, :, None] == targets[None, None, :]
    located = jnp.any(matches, axis=1)
    offset_in = jnp.sum(jnp.where(matches, (everyone % TPB)[:, :, None], 0), axis=1)
    return (located, offset_in)


def on_device(child_fronts, child_tiles, parent_front):
    row_count = lax.axis_size("row")
    col_count = lax.axis_size("col")
    row_ratio = row_count // col_count
    row_blocks = parent_front.shape[0] // PANEL
    col_blocks = parent_front.shape[1] // PANEL
    slot_count = row_blocks * col_blocks
    devices_all = row_count * col_count
    factor, update = eliminate_child(child_fronts[0])
    indices = child_tiles[0]
    block_ids = jnp.arange(NB, dtype=jnp.int32)
    matches = (indices // TPB)[None, :] == block_ids[:, None]
    present = jnp.any(matches, axis=1)
    source_tile = jnp.sum(jnp.where(matches, jnp.arange(CT, dtype=jnp.int32)[None, :], 0), axis=1)
    picked_rows = (
        source_tile[:, None] * TILE + jnp.arange(TILE, dtype=jnp.int32)[None, :]
    ).reshape(-1)
    spread = jnp.take(jnp.take(update, picked_rows, axis=0), picked_rows, axis=1)
    spread = spread.reshape(NB, TILE, NB, TILE)
    spread = jnp.where((present[:, None] & present[None, :])[:, None, :, None], spread, 0.0)
    outgoing = spread.reshape(row_count, row_blocks, TILE, col_count, col_blocks, TILE)
    outgoing = outgoing.transpose(0, 3, 1, 4, 2, 5).reshape(
        row_count, col_count, slot_count, TILE, TILE
    )
    arrived = lax.all_to_all(
        outgoing.reshape(devices_all, slot_count, TILE, TILE),
        ("row", "col"),
        split_axis=0,
        concat_axis=0,
        tiled=True,
    )
    arrived = arrived.reshape(devices_all * slot_count, TILE * TILE)
    everyone = lax.all_gather(child_tiles, ("row", "col"), axis=0, tiled=True)
    row_index = lax.axis_index("row")
    col_index = lax.axis_index("col")
    own_rows = row_index * row_blocks + jnp.arange(row_blocks, dtype=jnp.int32)
    own_cols = col_index * col_blocks + jnp.arange(col_blocks, dtype=jnp.int32)
    found_rows, offset_rows = locate(everyone, own_rows)
    found_cols, offset_cols = locate(everyone, own_cols)
    row_spot = jnp.arange(row_blocks, dtype=jnp.int32)[None, :] * TPB + offset_rows
    col_spot = jnp.arange(col_blocks, dtype=jnp.int32)[None, :] * TPB + offset_cols
    target_spots = row_spot[:, :, None] * (col_blocks * TPB) + col_spot[:, None, :]
    target_spots = jnp.where(
        found_rows[:, :, None] & found_cols[:, None, :], target_spots, -1
    ).reshape(-1)
    places = row_blocks * TPB * col_blocks * TPB
    chooser = (jnp.arange(places, dtype=jnp.int32)[:, None] == target_spots[None, :]).astype(
        jnp.float32
    )
    summed = jnp.dot(chooser, arrived, precision=PRECISE, preferred_element_type=jnp.float32)
    summed = summed.reshape(row_blocks * TPB, col_blocks * TPB, TILE, TILE).transpose(0, 2, 1, 3)
    assembled = parent_front + summed.reshape(parent_front.shape)
    identity = jnp.eye(PANEL, dtype=jnp.float32)
    for pivot_step in range(PANELS):
        row_slot = pivot_step % row_blocks
        col_slot = pivot_step % col_blocks
        owner_row = pivot_step // row_blocks
        owner_col = pivot_step // col_blocks
        column_block = assembled[:, col_slot * PANEL : (col_slot + 1) * PANEL]
        candidate = column_block
        holder = (row_index == owner_row) & (col_index == owner_col)
        candidate = jnp.where(holder, candidate, identity)
        corner = from_root(jnp.linalg.cholesky(candidate), "row", owner_row)
        panel_rows = keep_blocks(right_solve(corner, column_block), own_rows, pivot_step, corner)
        panel_rows = from_root(panel_rows, "col", owner_col)
        pieces = []
        for member in range(row_ratio):
            pieces.append(from_root(panel_rows, "row", col_index * row_ratio + member))
        panel_cols = jnp.concatenate(pieces, axis=0)
        change = product(panel_rows, panel_cols)
        row_live = jnp.repeat(own_rows > pivot_step, PANEL)
        col_live = jnp.repeat(own_cols > pivot_step, PANEL)
        row_here = jnp.repeat(own_rows == pivot_step, PANEL)
        col_here = jnp.repeat(own_cols == pivot_step, PANEL)
        renewed = jnp.where(row_live[:, None] & col_live[None, :], assembled - change, assembled)
        renewed = jnp.where(row_here[:, None] & col_live[None, :], 0.0, renewed)
        assembled = jnp.where(col_here[None, :], jnp.tile(panel_rows, (1, col_blocks)), renewed)
    return (factor[None], assembled)


def solution(mesh):
    placed = (P(("row", "col"), None, None), P(("row", "col"), None), P("row", "col"))
    return jax.shard_map(
        on_device,
        mesh=mesh,
        in_specs=placed,
        out_specs=(P(("row", "col"), None, None), P("row", "col")),
        check_vma=False,
    )
```

profile of v0, /device:TPU:1, one launch (start us, length us, event | category | flops | bytes accessed | tf_op | source)
XLA Modules:
  0.0 1473.4 jit_solution(17172467723713971530)
XLA Ops:
  7.2 17.6 %copy.75 = f32[1,2048,2048]{1,2,0:T(8,128)} copy(f32[1,2048,2048]{2,1,0:T(8,128)} %param.6) | data formatting | bytes 33554432 | tf_op args[0]
  35.0 11.7 cholesky.374
  46.7 9.8 custom-call.35
  60.8 11.7 cholesky.393
  73.2 10.0 custom-call.36
  85.5 11.7 cholesky.414
  98.6 9.8 custom-call.37
  110.7 12.1 cholesky.431
  130.1 11.2 while.5
  142.0 40.1 %custom-call.27 = f32[4,128,128]{1,2,0:T(8,128)S(1)} custom-call(f32[4,128,128]{2,1,0:T(8,128)} %copy-done.22), custom_call_target="InvertDiagBlocksLowerTriangular" | custom-call | tf_op jit(solution)/shard_map/jit(_solve_triangular)/triangular_solve | solution.py:34
  193.1 19.6 %slice_subtract_fusion = f32[1536,1536]{0,1:T(8,128)} fusion(f32[2048,2048]{0,1:T(8,128)} %bitcast.231, f32[128,1536]{1,0:T(8,128)S(1)} %fusion.93, f32[128,1536]{1,0:T(8,128)S(1)} %fusion.94, f32[128,1536]{1,0:T(8,128)S(1)} %fusion.96, f32[128,1536]{1,0:T(8,128)S(1)} %fusion.35), kind=kOutput, calls=%fused_computation.10 | convolution fusion | flops 14500233216 | bytes 22020096 | tf_op jit(solution)/shard_map/dot_general | solution.py:24
  212.6 9.6 copy.84
  222.2 18.0 %gather_fusion = f32[2048,1536]{1,0:T(8,128)} fusion(f32[1536,1536]{1,0:T(8,128)} %copy.84, s32[2048]{0:T(1024)S(1)} %broadcast_clamp_fusion), kind=kCustom, calls=%fused_computation | custom fusion | bytes 25174016 | tf_op jit(solution)/shard_map/jit(_take)/gather | solution.py:76
  240.2 10.0 broadcast_select_fusion
  250.2 12.6 copy.85
  262.7 21.1 %gather_fusion.1 = f32[2048,2048]{1,0:T(8,128)} fusion(f32[2048,1536]{0,1:T(8,128)} %copy.85, s32[2048]{0:T(1024)S(1)} %broadcast_clamp_fusion), kind=kCustom, calls=%fused_computation.1 | custom fusion | bytes 33562624 | tf_op jit(solution)/shard_map/jit(_take)/gather | solution.py:76
  283.8 14.2 copy.126
  298.0 17.7 %copy.86 = f32[16,1,128,8,2,128]{5,2,4,3,0,1:T(8,128)} copy(f32[16,1,128,8,2,128]{2,0,5,4,3,1:T(8,128)} %bitcast.226) | data formatting | bytes 33554432 | tf_op jit(solution)/shard_map/jit(_take)/gather | solution.py:76
  316.0 11.6 select_select_fusion
  327.6 11.9 all-to-all-start
  339.6 264.6 %all-gather = s32[128,1,12]{2,1,0:T(1,128)S(1)} all-gather(s32[1,1,12]{2,1,0:T(1,128)S(1)} %bitcast.237), channel_id=1, replica_groups=mesh['row'=16,'col'=8] {'row','col'}, dimensions={0}, use_global_device_ids=true | all-gather | bytes 6192 | tf_op jit(solution)/shard_map/all_gather | solution.py:91
  607.9 18.4 %copy.131 = f32[32,8,128,128]{3,1,2,0:T(8,128)} copy(f32[32,8,128,128]{3,2,1,0:T(8,128)} %bitcast.82) | data formatting | bytes 33554432
  626.3 17.5 %copy.87 = f32[16384,256]{1,0:T(8,128)} copy(f32[16384,256]{0,1:T(8,128)} %bitcast.227) | data formatting | bytes 33554432 | tf_op jit(solution)/shard_map/dot_general | solution.py:108
  643.8 11.2 fusion.110
  665.4 11.7 cholesky.446
  677.2 9.8 custom-call.38
  689.6 11.7 cholesky.465
  702.7 9.9 custom-call.39
  714.2 11.7 cholesky.486
  726.6 9.8 custom-call.40
  737.8 12.1 cholesky.503
  754.2 81.5 %all-reduce.10.cloned.1.call-done = f32[512,512]{1,0:T(8,128)} async-done(((f32[512,512]{1,0:T(8,128)}), f32[512,512]{1,0:T(8,128)}) %all-reduce.10.cloned.1.call-update) | async-done | bytes 1048592 | tf_op jit(solution)/shard_map/psum | solution.py:20
  838.1 11.2 while.6
  849.3 39.9 %custom-call.41 = f32[4,128,128]{1,2,0:T(8,128)} custom-call(f32[4,128,128]{2,1,0:T(8,128)S(1)} %get-tuple-element.26), custom_call_target="InvertDiagBlocksLowerTriangular" | custom-call | tf_op jit(solution)/shard_map/jit(_solve_triangular)/triangular_solve | solution.py:34
  907.4 61.0 %all-reduce.12.cloned.1.call-done = f32[512,512]{1,0:T(8,128)} async-done(((f32[512,512]{1,0:T(8,128)}), f32[512,512]{1,0:T(8,128)}) %all-reduce.12.cloned.1.call-update) | async-done | bytes 1048592 | tf_op jit(solution)/shard_map/psum | solution.py:20
  973.1 90.1 %all-reduce.20.cloned.1.call-done = (f32[512,512]{1,0:T(8,128)}, f32[512,512]{1,0:T(8,128)}) async-done(((f32[512,512]{1,0:T(8,128)}, f32[512,512]{1,0:T(8,128)}), (f32[512,512]{1,0:T(8,128)}, f32[512,512]{1,0:T(8,128)})) %all-reduce.20.cloned.1.call-update) | async-done | bytes 2097168 | tf_op jit(solution)/shard_map/psum | solution.py:20
  1071.9 11.7 cholesky.518
  1083.7 9.8 custom-call.42
  1096.1 11.9 cholesky.537
  1109.4 9.8 custom-call.43
  1120.8 11.7 cholesky.558
  1133.2 10.0 custom-call.44
  1144.6 11.7 cholesky.575
  1160.7 86.3 %all-reduce.14.cloned.1.call-done = f32[512,512]{1,0:T(8,128)} async-done(((f32[512,512]{1,0:T(8,128)}), f32[512,512]{1,0:T(8,128)}) %all-reduce.14.cloned.1.call-update) | async-done | bytes 1048592 | tf_op jit(solution)/shard_map/psum | solution.py:20
  1248.4 8.2 while.7
  1256.6 39.3 %custom-call.45 = f32[4,128,128]{1,2,0:T(8,128)S(1)} custom-call(f32[4,128,128]{2,1,0:T(8,128)S(1)} %get-tuple-element.27), custom_call_target="InvertDiagBlocksLowerTriangular" | custom-call | tf_op jit(solution)/shard_map/jit(_solve_triangular)/triangular_solve | solution.py:34
  1301.1 60.7 %all-reduce.16.cloned.1.call-done = f32[512,512]{1,0:T(8,128)} async-done(((f32[512,512]{1,0:T(8,128)}), f32[512,512]{1,0:T(8,128)}) %all-reduce.16.cloned.1.call-update) | async-done | bytes 1048592 | tf_op jit(solution)/shard_map/psum | solution.py:20
  1377.9 78.5 %all-reduce.18.cloned.1.call-done = (f32[512,512]{1,0:T(8,128)}, f32[512,512]{1,0:T(8,128)}) async-done(((f32[512,512]{1,0:T(8,128)}, f32[512,512]{1,0:T(8,128)}), (f32[512,512]{1,0:T(8,128)}, f32[512,512]{1,0:T(8,128)})) %all-reduce.18.cloned.1.call-update) | async-done | bytes 2097168 | tf_op jit(solution)/shard_map/psum | solution.py:20
  (266 shorter events, 167.0 us)
Async XLA Ops:
  27.1 2.1 copy-start.25
  34.0 1.0 copy-start.19
  141.3 0.7 copy-start.22
  142.0 45.6 %copy-start.23 = (s32[4,2]{0,1:T(2,128)}, s32[4,2]{0,1:T(2,128)S(1)}, u32[]{:S(2)}) copy-start(s32[4,2]{0,1:T(2,128)S(1)} %get-tuple-element.299) | copy-start | bytes 100
  183.0 9.1 copy-start
  185.6 6.5 copy-start.2
  188.5 3.6 copy-start.6
  192.1 0.9 copy-start.10
  327.6 278.4 %copy-start.21 = (f32[512,1024]{1,0:T(8,128)S(1)}, f32[512,1024]{1,0:T(8,128)}, u32[]{:S(2)}) copy-start(f32[512,1024]{1,0:T(8,128)} %param.8) | copy-start | bytes 6291460
  327.6 280.3 %all-to-all-start = ((f32[128,2,128,128]{3,2,1,0:T(8,128)}), f32[128,2,128,128]{3,2,1,0:T(8,128)}, u32[]{:S(2)}, u32[]{:S(2)}) async-start(f32[128,2,128,128]{3,2,1,0:T(8,128)} %bitcast.224), calls=%async_computation | async-start | bytes 33554432 | tf_op jit(solution)/shard_map/all_to_all | solution.py:83
  339.5 496.2 %all-reduce.10.cloned.1.call-start = ((), (), s32[]{:S(2)}) async-start(), calls=%async_computation.1 | async-start | bytes 2097152 | tf_op jit(solution)/shard_map/psum | solution.py:20
  664.4 1.0 copy-start.17
  725.9 112.1 %copy-start.24 = (s32[4,2]{0,1:T(2,128)S(1)}, s32[4,2]{0,1:T(2,128)}, u32[]{:S(2)}) copy-start(s32[4,2]{0,1:T(2,128)} %copy-done.23) | copy-start | bytes 100
  754.2 135.1 %copy-start.14 = (f32[512,512]{1,0:T(8,128)S(1)}, f32[512,512]{1,0:T(8,128)}, u32[]{:S(2)}) copy-start(f32[512,512]{1,0:T(8,128)} %get-tuple-element.78) | copy-start | bytes 3145732
  754.2 214.2 %all-reduce.12.cloned.1.call-start = ((), (), s32[]{:S(2)}) async-start(), calls=%async_computation.2 | async-start | bytes 2097152 | tf_op jit(solution)/shard_map/psum | solution.py:20
  891.7 13.3 copy-start.13
  893.1 2.8 copy-start.15
  895.9 0.7 copy-start.20
  907.4 155.8 %all-reduce.20.cloned.1.call-start = ((), (), s32[]{:S(2)}) async-start(), calls=%async_computation.6 | async-start | bytes 4194304 | tf_op jit(solution)/shard_map/psum | solution.py:20
  968.4 3.3 copy-start.9
  971.4 275.7 %all-reduce.14.cloned.1.call-start = ((), (), s32[]{:S(2)}) async-start(), calls=%async_computation.3 | async-start | bytes 2097152 | tf_op jit(solution)/shard_map/psum | solution.py:20
  1068.7 1.3 copy-start.4
  1070.9 1.0 copy-start.18
  1160.6 201.2 %all-reduce.16.cloned.1.call-start = ((), (), s32[]{:S(2)}) async-start(), calls=%async_computation.4 | async-start | bytes 2097152 | tf_op jit(solution)/shard_map/psum | solution.py:20
  1298.0 1.5 copy-start.12
  1300.8 66.8 %copy-start.1 = (f32[128,1536]{1,0:T(8,128)S(1)}, f32[128,1536]{1,0:T(8,128)}, u32[]{:S(2)}) copy-start(f32[128,1536]{1,0:T(8,128)} %copy-done) | copy-start | bytes 2359300
  1300.8 66.8 %copy-start.3 = (f32[128,1536]{1,0:T(8,128)S(1)}, f32[128,1536]{1,0:T(8,128)}, u32[]{:S(2)}) copy-start(f32[128,1536]{1,0:T(8,128)} %copy-done.2) | copy-start | bytes 2359300
  1300.8 66.8 %copy-start.7 = (f32[128,1536]{1,0:T(8,128)S(1)}, f32[128,1536]{1,0:T(8,128)}, u32[]{:S(2)}) copy-start(f32[128,1536]{1,0:T(8,128)} %copy-done.6) | copy-start | bytes 2359300
  1300.8 66.7 %copy-start.11 = (f32[128,1536]{1,0:T(8,128)S(1)}, f32[128,1536]{1,0:T(8,128)}, u32[]{:S(2)}) copy-start(f32[128,1536]{1,0:T(8,128)} %copy-done.10) | copy-start | bytes 2359300
  1300.8 155.5 %all-reduce.18.cloned.1.call-start = ((), (), s32[]{:S(2)}) async-start(), calls=%async_computation.5 | async-start | bytes 4194304 | tf_op jit(solution)/shard_map/psum | solution.py:20
  1367.6 1.2 copy-start.16
  1371.1 5.4 copy-start.8
  1376.5 79.8 %copy-start.5 = (f32[512,1024]{0,1:T(8,128)S(1)}, f32[512,1024]{0,1:T(8,128)}, u32[]{:S(2)}) copy-start(f32[512,1024]{0,1:T(8,128)} %copy-done.4) | copy-start | bytes 6291460
Sparse Core Ops, SparseCore 0:
  754.3 81.3 all-reduce.9
  907.5 60.8 all-reduce.11
  972.4 90.7 all-reduce.19
  1160.8 86.2 all-reduce.13
  1300.9 60.8 all-reduce.15
  1365.4 90.8 all-reduce.17
where the time goes:
time: 1490 us; the launch traced here: 1470 us
  waiting for transfers between devices  458 us (31%)
  other arithmetic  410 us (28%)
  blocking collectives  265 us (18%)
  local copies, waits for them, and re-layouts  219 us (15%)
  matrix products  85.5 us (6%)
  between operations  23 us (2%)
    psum x6, waiting for transfers between devices, from_root(): return lax.psum(kept, axis)  458 us
    all_gather x1, blocking collectives, on_device(): everyone = lax.all_gather(child_tiles, ('row', 'col'), axis=0, tiled=True)  265 us
    another operation x30, other arithmetic, on_device(): corner = from_root(jnp.linalg.cholesky(candidate), 'row', owner_row)  159 us
    another operation x7, other arithmetic, right_solve(): jax.scipy.linalg.solve_triangular(factor, right_block.T, lower=True)  126 us
    another operation x14, other arithmetic, eliminate_child(): corner = jnp.linalg.cholesky(matrix[:CP, :CP])  80.8 us
    unnamed x62, local copies, waits for them, and re-layouts  68.5 us
    gather x2, local copies, waits for them, and re-layouts, on_device(): jnp.take(jnp.take(update, picked_rows, axis=0), picked_rows, axis=1)  38.8 us
    dot_general x3, matrix products, product(): lax.dot_general(left_side, right_side, (((1,), (1,)), ((), ())), precisio...  32.1 us
  transfers between devices with their start and end apart: 7, of which 6 were waited for; matrix products, arithmetic and copies ran while one was open for 1% of the time, Pallas kernels for 0%

commit v1 on v0

v1 whole, which is shorter than its diff:
```python
import functools

import jax
import jax.numpy as jnp
from jax import lax
from jax.experimental import pallas as pl
from jax.experimental.pallas import tpu as pltpu
from jax.sharding import PartitionSpec as P

PANEL = 512
TILE = 128
CP = 512
CW = 2048
CT = 12
REST = CW - CP
PIV = 1024
DEV = 128
PAIRS = CT * (CT + 1) // 2
SLOTS = 80
META = PAIRS
AXES = ("row", "col")
PRECISE = lax.Precision.HIGHEST
VMEM = 56 * 1024 * 1024

pair_slot = {}
for _i in range(CT):
    for _j in range(_i + 1):
        pair_slot[_i, _j] = len(pair_slot)

corner_slot = {}
for _i in range(8):
    for _j in range(_i + 1):
        corner_slot[_i, _j] = len(corner_slot)
CORNER = 40
BACK = 128


def dot_t(x, y):
    return lax.dot_general(
        x, y, (((1,), (1,)), ((), ())), precision=PRECISE, preferred_element_type=jnp.float32
    )


def split(x):
    high = x.astype(jnp.bfloat16)
    return high, (x - high.astype(jnp.float32)).astype(jnp.bfloat16)


def dot_split(x, y):
    dims = (((1,), (1,)), ((), ()))
    f = functools.partial(lax.dot_general, dimension_numbers=dims, preferred_element_type=jnp.float32)
    return f(x[0], y[0]) + (f(x[0], y[1]) + f(x[1], y[0]))


def inverse_factor(tile):
    shape = (8, TILE)
    lane = lax.broadcasted_iota(jnp.int32, shape, 1)
    sub = lax.broadcasted_iota(jnp.int32, shape, 0)
    full = lambda v: jnp.broadcast_to(v, shape)
    rows = [tile[8 * k : 8 * k + 8, :] for k in range(16)]
    out = []
    for k in range(16):
        base = 8 * k
        columns = [[full(rows[q][:, base + m : base + m + 1]) for m in range(8)] for q in range(k, 16)]
        a = [[full(columns[0][n][m : m + 1, :]) if n >= m else None for n in range(8)] for m in range(8)]
        inside = (lane >= base) & (lane < base + 8)
        own = jnp.where(inside, jnp.where(lane - base == sub, 1.0, 0.0), rows[k])
        v = [full(own[m : m + 1, :]) for m in range(8)]
        w = []
        for m in range(8):
            r = 1.0 / a[m][m]
            g = [a[m][n] * r if n > m else None for n in range(8)]
            for n in range(m + 1, 8):
                for p in range(n, 8):
                    a[n][p] = a[n][p] - g[n] * a[m][p]
            for n in range(m + 1, 8):
                v[n] = v[n] - g[n] * v[m]
            w.append(v[m] * r)
            for q in range(1, 16 - k):
                for n in range(m + 1, 8):
                    columns[q][n] = columns[q][n] - columns[q][m] * g[n]
        for q in range(1, 16 - k):
            terms = [columns[q][m] * w[m] for m in range(8)]
            while len(terms) > 1:
                terms = [terms[t] + terms[t + 1] for t in range(0, len(terms), 2)]
            rows[k + q] = jnp.where(inside, 0.0, rows[k + q]) - terms[0]
        mine, scale = v[0], a[0][0]
        for m in range(1, 8):
            mine = jnp.where(sub == m, v[m], mine)
            scale = jnp.where(sub == m, a[m][m], scale)
        out.append(jnp.where(lane <= base + sub, mine * lax.rsqrt(scale), 0.0))
    return jnp.concatenate(out, axis=0)


def factor_blocks(a_ref, l_ref, inv_ref, order):
    count = order // TILE
    tri = lax.broadcasted_iota(jnp.int32, (TILE, TILE), 0) >= lax.broadcasted_iota(
        jnp.int32, (TILE, TILE), 1
    )

    def step(kb, _):
        at = pl.multiple_of(kb * TILE, TILE)
        inverse = inverse_factor(a_ref[pl.ds(at, TILE), pl.ds(at, TILE)])
        inv_ref[pl.ds(at, TILE), :] = inverse
        for q in range(count):

            @pl.when(kb == q)
            def _():
                lo = q * TILE
                panel = dot_t(a_ref[lo:order, lo : lo + TILE], inv_ref[lo : lo + TILE, :])
                l_ref[lo : lo + TILE, lo : lo + TILE] = jnp.where(tri, panel[:TILE], 0.0)
                if q + 1 < count:
                    l_ref[lo + TILE : order, lo : lo + TILE] = panel[TILE:]
                    for j in range(q + 1, count):
                        left = panel[(j - q) * TILE :]
                        a_ref[j * TILE : order, j * TILE : (j + 1) * TILE] = a_ref[
                            j * TILE : order, j * TILE : (j + 1) * TILE
                        ] - dot_t(left, left[:TILE])

        return 0

    lax.fori_loop(0, count, step, 0)


def child_kernel(tiles_ref, front_ref, factor_ref, out_ref, a_ref, b_ref, c_ref, inv_ref, hi_ref, lo_ref, sems):
    copy_a = pltpu.make_async_copy(front_ref.at[pl.ds(0, CP), pl.ds(0, CP)], a_ref, sems.at[0])
    copy_b = pltpu.make_async_copy(front_ref.at[pl.ds(CP, REST), pl.ds(0, CP)], b_ref, sems.at[1])
    copy_c = pltpu.make_async_copy(front_ref.at[pl.ds(CP, REST), pl.ds(CP, REST)], c_ref, sems.at[2])
    copy_a.start()
    copy_b.start()
    copy_c.start()
    copy_a.wait()
    factor_ref[0:CP, :] = jnp.zeros((CP, CP), jnp.float32)
    factor_blocks(a_ref, factor_ref, inv_ref, CP)
    copy_b.wait()
    for kb in range(CP // TILE):
        lo = kb * TILE
        part = b_ref[:, lo : lo + TILE]
        if kb:
            part = part - dot_split(
                (hi_ref[:, :lo], lo_ref[:, :lo]), split(factor_ref[lo : lo + TILE, :lo])
            )
        part = dot_t(part, inv_ref[lo : lo + TILE, :])
        factor_ref[CP:CW, lo : lo + TILE] = part
        high, low = split(part)
        hi_ref[:, lo : lo + TILE] = high
        lo_ref[:, lo : lo + TILE] = low
    copy_c.wait()
    for i in range(CT):
        rows = slice(i * TILE, (i + 1) * TILE)
        wide = (i + 1) * TILE
        update = c_ref[rows, :wide] - dot_split(
            (hi_ref[rows, :], lo_ref[rows, :]), (hi_ref[:wide, :], lo_ref[:wide, :])
        )
        for j in range(i + 1):
            out_ref[pl.ds(pair_slot[i, j], DEV, stride=SLOTS), :] = update[:, j * TILE : (j + 1) * TILE]
    meta = jnp.broadcast_to(tiles_ref[0:1, :], (DEV, TILE))
    out_ref[pl.ds(META, DEV, stride=SLOTS), :] = meta
    out_ref[pl.ds(META + 1, DEV, stride=SLOTS), :] = meta


def eliminate_child(front, tiles):
    spec = pl.BlockSpec(memory_space=pltpu.VMEM)
    return pl.pallas_call(
        child_kernel,
        out_shape=(
            jax.ShapeDtypeStruct((CW, CP), jnp.float32),
            jax.ShapeDtypeStruct((DEV * SLOTS, TILE), jnp.float32),
        ),
        in_specs=[spec, pl.BlockSpec(memory_space=pl.ANY)],
        out_specs=(spec, spec),
        scratch_shapes=[
            pltpu.VMEM((CP, CP), jnp.float32),
            pltpu.VMEM((REST, CP), jnp.float32),
            pltpu.VMEM((REST, REST), jnp.float32),
            pltpu.VMEM((CP, TILE), jnp.float32),
            pltpu.VMEM((REST, CP), jnp.bfloat16),
            pltpu.VMEM((REST, CP), jnp.bfloat16),
            pltpu.SemaphoreType.DMA((3,)),
        ],
        compiler_params=pltpu.CompilerParams(vmem_limit_bytes=VMEM),
        cost_estimate=pl.CostEstimate(flops=12 * 10**9, bytes_accessed=30 * 10**6, transcendentals=0),
        name="child",
    )(tiles, front)


def sum_kernel(parent_ref, in_ref, corner_ref, back_ref, acc_ref, meta_ref, pack_ref, table_ref, sem):
    acc_ref[0 : DEV * 32, :] = parent_ref[...]
    ids = in_ref[pl.ds(META, DEV, stride=SLOTS), :].astype(jnp.int32)
    as_row = (ids // 4) * 256 + (ids % 4) * 8
    as_col = (ids // 8) * 32 + ids % 8
    lane = lax.broadcasted_iota(jnp.int32, (DEV, TILE), 1)
    meta_ref[...] = jnp.where(lane < 64, as_row, pltpu.roll(as_col, 64, axis=1))
    copy = pltpu.make_async_copy(meta_ref, table_ref, sem)
    copy.start()
    copy.wait()

    def add_child(s, _):
        base = s * SLOTS
        row_of = [table_ref[s, i] for i in range(CT)]
        col_of = [table_ref[s, 64 + j] for j in range(CT)]
        todo = list(pair_slot.items())
        for first in range(0, PAIRS, 26):
            group = todo[first : first + 26]
            places = [row_of[i] + col_of[j] for (i, j), _ in group]
            sums = [
                acc_ref[pl.ds(place, 1), :] + in_ref[pl.ds(base + slot, 1), :]
                for place, (_, slot) in zip(places, group)
            ]
            for place, total in zip(places, sums):
                acc_ref[pl.ds(place, 1), :] = total
        return 0

    lax.fori_loop(0, DEV, add_child, 0)

    for (i, j), slot in corner_slot.items():
        place = (i // 4) * 256 + (i % 4) * 8 + j
        pack_ref[slot : slot + 1, :] = acc_ref[place : place + 1, :]
    for slot in range(len(corner_slot), CORNER):
        pack_ref[slot : slot + 1, :] = jnp.zeros((1, TILE), jnp.float32)
    pack = pack_ref[...]
    sub = lax.broadcasted_iota(jnp.int32, (8, TILE), 0)

    def pack_device(g, _):
        corner_ref[pl.ds(pl.multiple_of(g * CORNER, 8), CORNER), :] = pack
        r = g // 8
        c = g % 8
        base = pl.multiple_of(g * BACK, 8)
        odd = (r % 2) == 1
        first = jnp.where(sub < 4, 0, 1) + 2 * c <= r
        for k in range(4):
            lower = acc_ref[pl.ds(pl.multiple_of(g * 32 + k * 8, 8), 8), :]
            m0 = acc_ref[pl.ds(pl.multiple_of(((2 * c) * 8 + r // 2) * 32 + k * 8, 8), 8), :]
            m1 = acc_ref[pl.ds(pl.multiple_of(((2 * c + 1) * 8 + r // 2) * 32 + k * 8, 8), 8), :]
            m0 = jnp.where(odd, pltpu.roll(m0, 4, axis=0), m0)
            m1 = jnp.where(odd, m1, pltpu.roll(m1, 4, axis=0))
            upper = jnp.where(sub < 4, m0, m1)
            back_ref[pl.ds(base + k * 8, 8), :] = jnp.where(first, lower, upper)
        back_ref[pl.ds(base + 32, 32), :] = acc_ref[pl.ds(pl.multiple_of(r * 256, 8), 32), :]
        back_ref[pl.ds(base + 64, 32), :] = acc_ref[pl.ds(pl.multiple_of(c * 512, 8), 32), :]
        back_ref[pl.ds(base + 96, 32), :] = acc_ref[pl.ds(pl.multiple_of(c * 512 + 256, 8), 32), :]
        return 0

    lax.fori_loop(0, DEV, pack_device, 0)


def sum_slices(parent, arrived):
    spec = pl.BlockSpec(memory_space=pltpu.VMEM)
    return pl.pallas_call(
        sum_kernel,
        out_shape=(
            jax.ShapeDtypeStruct((DEV * CORNER, TILE), jnp.float32),
            jax.ShapeDtypeStruct((DEV * BACK, TILE), jnp.float32),
        ),
        in_specs=[spec, spec],
        out_specs=(spec, spec),
        scratch_shapes=[
            pltpu.VMEM((DEV * 32, TILE), jnp.float32),
            pltpu.VMEM((DEV, TILE), jnp.int32),
            pltpu.VMEM((CORNER, TILE), jnp.float32),
            pltpu.SMEM((DEV, TILE), jnp.int32),
            pltpu.SemaphoreType.DMA,
        ],
        compiler_params=pltpu.CompilerParams(vmem_limit_bytes=VMEM),
        name="sum_slices",
    )(parent, arrived)


def corner_kernel(in_ref, l_ref, inv_ref, a_ref):
    for (i, j), slot in corner_slot.items():
        a_ref[i * TILE : (i + 1) * TILE, j * TILE : (j + 1) * TILE] = in_ref[
            pl.ds(slot, DEV, stride=CORNER), :
        ]
    l_ref[...] = jnp.zeros((PIV, PIV), jnp.float32)
    factor_blocks(a_ref, l_ref, inv_ref, PIV)


def factor_corner(arrived):
    spec = pl.BlockSpec(memory_space=pltpu.VMEM)
    return pl.pallas_call(
        corner_kernel,
        out_shape=(
            jax.ShapeDtypeStruct((PIV, PIV), jnp.float32),
            jax.ShapeDtypeStruct((PIV, TILE), jnp.float32),
        ),
        in_specs=[spec],
        out_specs=(spec, spec),
        scratch_shapes=[pltpu.VMEM((PIV, PIV), jnp.float32)],
        compiler_params=pltpu.CompilerParams(vmem_limit_bytes=VMEM),
        cost_estimate=pl.CostEstimate(flops=70 * 10**9, bytes_accessed=10**7, transcendentals=0),
        name="corner",
    )(arrived)


def finish_kernel(where_ref, in_ref, l_ref, inv_ref, out_ref, x_ref, hi_ref, lo_ref):
    r = where_ref[0]
    c = where_ref[1]
    tile = lambda slot: in_ref[pl.ds(slot, DEV, stride=BACK), :]
    rows = 3 * PANEL

    @pl.when(r >= 2)
    def _():
        for a in range(CT):
            for j in range(8):
                x_ref[a * TILE : (a + 1) * TILE, j * TILE : (j + 1) * TILE] = tile(32 + a * 8 + j)
        for kb in range(PIV // TILE):
            lo = kb * TILE
            part = x_ref[:, lo : lo + TILE]
            if kb:
                part = part - dot_split(
                    (hi_ref[:, :lo], lo_ref[:, :lo]), split(l_ref[lo : lo + TILE, :lo])
                )
            part = dot_t(part, inv_ref[lo : lo + TILE, :])
            x_ref[:, lo : lo + TILE] = part
            high, low = split(part)
            hi_ref[:, lo : lo + TILE] = high
            lo_ref[:, lo : lo + TILE] = low

    @pl.when((r >= 2) & (c >= 1))
    def _():
        for q in range(2):
            cols = slice(PANEL * (q + 1), PANEL * (q + 2))
            out_ref[:, q * PANEL : (q + 1) * PANEL] = dot_split(
                (hi_ref[:PANEL, :], lo_ref[:PANEL, :]), (hi_ref[cols, :], lo_ref[cols, :])
            )
            for a in range(4):
                for b in range(4):
                    spot = (slice(a * TILE, (a + 1) * TILE), slice(q * PANEL + b * TILE, q * PANEL + (b + 1) * TILE))
                    mirrored = (r < 2 * c + q) | ((r == 2 * c + q) & (a < b))

                    @pl.when(mirrored)
                    def _():
                        out_ref[spot] = tile(b * 8 + q * 4 + a).T - out_ref[spot]

                    @pl.when(jnp.logical_not(mirrored))
                    def _():
                        out_ref[spot] = tile(a * 8 + q * 4 + b) - out_ref[spot]

    @pl.when((r >= 2) & (c == 0))
    def _():
        out_ref[...] = x_ref[:PANEL, :]

    @pl.when((r < 2) & (c == 0))
    def _():
        out_ref[...] = l_ref[pl.ds(pl.multiple_of(r * PANEL, PANEL), PANEL), :]

    @pl.when((r < 2) & (c >= 1))
    def _():
        out_ref[...] = jnp.zeros((PANEL, PIV), jnp.float32)


def finish(where, arrived, corner, inverses):
    spec = pl.BlockSpec(memory_space=pltpu.VMEM)
    rows = 3 * PANEL
    return pl.pallas_call(
        finish_kernel,
        out_shape=jax.ShapeDtypeStruct((PANEL, PIV), jnp.float32),
        in_specs=[pl.BlockSpec(memory_space=pltpu.SMEM), spec, spec, spec],
        out_specs=spec,
        scratch_shapes=[
            pltpu.VMEM((rows, PIV), jnp.float32),
            pltpu.VMEM((rows, PIV), jnp.bfloat16),
            pltpu.VMEM((rows, PIV), jnp.bfloat16),
        ],
        compiler_params=pltpu.CompilerParams(vmem_limit_bytes=VMEM),
        name="finish",
    )(where, arrived, corner, inverses)


def exchange(x):
    y = x.reshape(DEV, x.shape[0] // DEV, TILE)
    return lax.all_to_all(y, AXES, 0, 0, tiled=True).reshape(x.shape)


def on_device(child_fronts, child_tiles, parent_front):
    row = lax.axis_index("row")
    col = lax.axis_index("col")
    parent = parent_front.reshape(4, TILE, 8, TILE).transpose(1, 0, 2, 3).reshape(DEV * 32, TILE)
    parent = exchange(parent)
    tiles = jnp.pad(child_tiles.astype(jnp.float32), ((0, 7), (0, TILE - CT)))
    factor, outgoing = eliminate_child(child_fronts[0], tiles)
    corner_rows, back_rows = sum_slices(parent, exchange(outgoing))
    corner, inverses = factor_corner(exchange(corner_rows))
    where = jnp.stack([row, col]).astype(jnp.int32)
    result = finish(where, exchange(back_rows), corner, inverses)
    return factor[None], result


def solution(mesh):
    placed = (P(AXES, None, None), P(AXES, None), P("row", "col"))
    return jax.shard_map(
        on_device,
        mesh=mesh,
        in_specs=placed,
        out_specs=(P(AXES, None, None), P("row", "col")),
        check_vma=False,
    )
```

time: 1490 us -> 355 us (0.24)
  the two profiles are of different devices: /device:TPU:1 before, /device:TPU:26 now
where the time goes in v1:
time: 355 us; the launch traced here: 349 us
  Pallas kernels  163 us (46%)
  blocking collectives  112 us (32%)
  waiting for transfers between devices  48.4 us (14%)
  starting transfers between devices  19.6 us (6%)
  local copies, waits for them, and re-layouts  4.28 us (1%)
    all_to_all x2, blocking collectives, exchange(): return lax.all_to_all(y, AXES, 0, 0, tiled=True).reshape(x.shape)  112 us
    pallas_call x1, Pallas kernels, factor_corner(): pl.pallas_call(corner_kernel, out_shape=(jax.ShapeDtypeStruct((PIV, PIV),...  53.1 us
    all_to_all x2, waiting for transfers between devices, exchange(): return lax.all_to_all(y, AXES, 0, 0, tiled=True).reshape(x.shape)  48.4 us
    pallas_call x1, Pallas kernels, eliminate_child(): pl.pallas_call(child_kernel, out_shape=(jax.ShapeDtypeStruct((CW, CP), jn...  44.5 us
    pallas_call x1, Pallas kernels, finish(): pl.pallas_call(finish_kernel, out_shape=jax.ShapeDtypeStruct((PANEL, PIV)...  40 us
    pallas_call x1, Pallas kernels, sum_slices(): pl.pallas_call(sum_kernel, out_shape=(jax.ShapeDtypeStruct((DEV * CORNER,...  25.2 us
    all_to_all x2, starting transfers between devices, exchange(): return lax.all_to_all(y, AXES, 0, 0, tiled=True).reshape(x.shape)  19.6 us
  transfers between devices with their start and end apart: 2, of which 1 were waited for; matrix products, arithmetic and copies ran while one was open for 0% of the time, Pallas kernels for 28%

profile of v1, /device:TPU:26, one launch (start us, length us, event | category | flops | bytes accessed | tf_op | source)
XLA Modules:
  0.0 348.9 jit_solution(16470169928392240481)
XLA Ops:
  0.6 2.1 copy.6
  2.7 1.6 copy_bitcast_fusion
  4.3 0.0 copy-start.1
  4.3 10.3 %all-to-all-start = ((f32[128,32,128]{2,1,0:T(8,128)}), f32[128,32,128]{2,1,0:T(8,128)S(1)}, u32[]{:S(2)}, u32[]{:S(2)}) async-start(f32[128,32,128]{2,1,0:T(8,128)} %copy_bitcast_fusion), calls=%async_computation | async-start | bytes 4194304 | tf_op jit(solution)/shard_map/all_to_all | solution.py:372
  14.6 0.0 copy-done.1
  14.6 0.6 pad.4.tiles_ref
  15.2 44.5 %child.1 = (f32[2048,512]{1,0:T(8,128)}, f32[10240,128]{1,0:T(8,128)}) custom-call(f32[8,128]{1,0:T(8,128)} %pad.4.tiles_ref, f32[2048,2048]{1,0:T(8,128)} %bitcast.31), custom_call_target="tpu_custom_call" | custom-call | flops 12000000000 | bytes 30000000 | tf_op jit(solution)/shard_map/child/pallas_call | solution.py:164
  59.7 0.0 all-to-all-done
  59.7 0.0 copy-start
  59.7 70.8 %all_to_all.20 = f32[128,80,128]{2,1,0:T(8,128)} all-to-all(f32[128,80,128]{2,1,0:T(8,128)} %bitcast.27), channel_id=1, replica_groups=mesh['row'=16,'col'=8] {'row','col'}, dimensions={0} | all-to-all | bytes 10485760 | tf_op jit(solution)/shard_map/all_to_all | solution.py:372
  130.5 0.0 copy-done
  130.5 25.2 %sum_slices.1 = (f32[5120,128]{1,0:T(8,128)}, f32[16384,128]{1,0:T(8,128)}) custom-call(f32[4096,128]{1,0:T(8,128)} %bitcast.24, f32[10240,128]{1,0:T(8,128)} %bitcast.23), custom_call_target="tpu_custom_call" | custom-call | tf_op jit(solution)/shard_map/sum_slices/pallas_call | solution.py:249
  155.7 41.3 %all_to_all.21 = f32[128,40,128]{2,1,0:T(8,128)} all-to-all(f32[128,40,128]{2,1,0:T(8,128)} %bitcast.29), channel_id=1, replica_groups=mesh['row'=16,'col'=8] {'row','col'}, dimensions={0} | all-to-all | bytes 5242880 | tf_op jit(solution)/shard_map/all_to_all | solution.py:372
  197.1 9.3 %all-to-all-start.2 = ((f32[128,128,128]{2,1,0:T(8,128)}), f32[128,128,128]{2,1,0:T(8,128)}, u32[]{:S(2)}, u32[]{:S(2)}) async-start(f32[128,128,128]{2,1,0:T(8,128)} %bitcast.25), calls=%async_computation.2 | async-start | bytes 16777216 | tf_op jit(solution)/shard_map/all_to_all | solution.py:372
  206.4 0.7 pad_add_fusion.where_ref
  207.1 53.1 %corner.1 = (f32[1024,1024]{1,0:T(8,128)}, f32[1024,128]{1,0:T(8,128)}) custom-call(f32[5120,128]{1,0:T(8,128)} %bitcast.28), custom_call_target="tpu_custom_call" | custom-call | flops 70000001024 | bytes 10000000 | tf_op jit(solution)/shard_map/corner/pallas_call | solution.py:280
  260.2 48.4 %all-to-all-done.2 = f32[128,128,128]{2,1,0:T(8,128)} async-done(((f32[128,128,128]{2,1,0:T(8,128)}), f32[128,128,128]{2,1,0:T(8,128)}, u32[]{:S(2)}, u32[]{:S(2)}) %all-to-all-start.2) | async-done | bytes 8388640 | tf_op jit(solution)/shard_map/all_to_all | solution.py:372
  308.6 40.0 %finish.1 = f32[512,1024]{1,0:T(8,128)} custom-call(s32[2]{0:T(128)} %pad_add_fusion.where_ref, f32[16384,128]{1,0:T(8,128)} %bitcast.10.in_ref, f32[1024,1024]{1,0:T(8,128)} %get-tuple-element.12.l_ref, f32[1024,128]{1,0:T(8,128)} %get-tuple-element.13.inv_ref), custom_call_target="tpu_custom_call" | custom-call | tf_op jit(solution)/shard_map/finish/pallas_call | solution.py:355
  (1 shorter events, 0.0 us)
Async XLA Ops:
  4.3 10.3 %copy-start.1 = (s32[1,12]{1,0:T(1,128)S(1)}, s32[1,12]{1,0:T(1,128)}, u32[]{:S(2)}) copy-start(s32[1,12]{1,0:T(1,128)} %param.4) | copy-start | bytes 148
  4.3 55.4 %all-to-all-start = ((f32[128,32,128]{2,1,0:T(8,128)}), f32[128,32,128]{2,1,0:T(8,128)S(1)}, u32[]{:S(2)}, u32[]{:S(2)}) async-start(f32[128,32,128]{2,1,0:T(8,128)} %copy_bitcast_fusion), calls=%async_computation | async-start | bytes 4194304 | tf_op jit(solution)/shard_map/all_to_all | solution.py:372
  59.7 70.8 %copy-start = (f32[128,32,128]{2,1,0:T(8,128)}, f32[128,32,128]{2,1,0:T(8,128)S(1)}, u32[]{:S(2)}) copy-start(f32[128,32,128]{2,1,0:T(8,128)S(1)} %all-to-all-done) | copy-start | bytes 6291460
  197.1 111.6 %all-to-all-start.2 = ((f32[128,128,128]{2,1,0:T(8,128)}), f32[128,128,128]{2,1,0:T(8,128)}, u32[]{:S(2)}, u32[]{:S(2)}) async-start(f32[128,128,128]{2,1,0:T(8,128)} %bitcast.25), calls=%async_computation.2 | async-start | bytes 16777216 | tf_op jit(solution)/shard_map/all_to_all | solution.py:372

commit v2 on v1

v2 whole, which is shorter than its diff:
```python
import functools

import jax
import jax.numpy as jnp
from jax import lax
from jax.experimental import pallas as pl
from jax.experimental.pallas import tpu as pltpu
from jax.sharding import PartitionSpec as P

PANEL = 512
TILE = 128
CP = 512
CW = 2048
CT = 12
REST = CW - CP
PIV = 1024
DEV = 128
PAIRS = CT * (CT + 1) // 2
AXES = ("row", "col")
PRECISE = lax.Precision.HIGHEST
VMEM = 56 * 1024 * 1024

SLOTS = 80
META = PAIRS
CHUNKS = 4

pair_slot = {}
for _i in range(CT):
    for _j in range(_i + 1):
        pair_slot[_i, _j] = len(pair_slot)

corner_slot = {}
for _i in range(8):
    for _j in range(_i + 1):
        corner_slot[_i, _j] = len(corner_slot)
HALF = 24
BACK = 80
BLOCK = 32
WIDE = 2 * TILE


def dot_t(x, y):
    return lax.dot_general(
        x, y, (((1,), (1,)), ((), ())), precision=PRECISE, preferred_element_type=jnp.float32
    )


def dot(x, y):
    return lax.dot_general(
        x, y, (((1,), (0,)), ((), ())), precision=PRECISE, preferred_element_type=jnp.float32
    )


def split(x):
    high = x.astype(jnp.bfloat16)
    return high, (x - high.astype(jnp.float32)).astype(jnp.bfloat16)


def dot_split(x, y):
    dims = (((1,), (1,)), ((), ()))
    f = functools.partial(lax.dot_general, dimension_numbers=dims, preferred_element_type=jnp.float32)
    return f(x[0], y[0]) + (f(x[0], y[1]) + f(x[1], y[0]))


def total(terms):
    while len(terms) > 1:
        terms = [terms[t] + terms[t + 1] for t in range(0, len(terms), 2)]
    return terms[0]


SPREAD = 256


def inverse_factor(tile, s_ref):
    shape = (8, TILE)
    lane = lax.broadcasted_iota(jnp.int32, shape, 1)
    sub = lax.broadcasted_iota(jnp.int32, shape, 0)
    column = lambda row, at: jnp.broadcast_to(row[:, at : at + 1], shape)
    spread = lambda at: s_ref[pl.ds(at, 8, stride=0), :]
    rows = [tile[8 * k : 8 * k + 8, :] for k in range(16)]
    out = []
    first = [column(rows[0], m) for m in range(8)]
    for k in range(16):
        base = 8 * k
        at = (k % 2) * 72
        columns = [first] + [[column(rows[q], base + m) for m in range(8)] for q in range(k + 1, 16)]
        if k < 15:
            first = [column(rows[k + 1], base + 8 + m) for m in range(8)]
        inside = (lane >= base) & (lane < base + 8)
        for m in range(8):
            s_ref[at + 8 * m : at + 8 * m + 8, :] = columns[0][m]
        s_ref[at + 64 : at + 72, :] = jnp.where(
            inside, jnp.where(lane - base == sub, 1.0, 0.0), rows[k]
        )
        v = [spread(at + 64 + m) for m in range(8)]
        a = [[spread(at + 8 * n + m) if n >= m else None for n in range(8)] for m in range(8)]
        w = []
        inverses = []
        for m in range(8):
            r = 1.0 / a[m][m]
            inverses.append(r)
            g = [a[m][n] * r if n > m else None for n in range(8)]
            for n in range(m + 1, 8):
                for p in range(n, 8):
                    a[n][p] = a[n][p] - g[n] * a[m][p]
            for n in range(m + 1, 8):
                v[n] = v[n] - g[n] * v[m]
            w.append(v[m] * r)
            for q in range(1, 16 - k):
                for n in range(m + 1, 8):
                    columns[q][n] = columns[q][n] - columns[q][m] * g[n]
        if k < 15:
            for m in range(8):
                s_ref[144 + 8 * m : 152 + 8 * m, :] = columns[1][m] * inverses[m]
            for n in range(8):
                first[n] = first[n] - total([columns[1][m] * spread(144 + 8 * m + n) for m in range(8)])
        for q in range(1, 16 - k):
            rows[k + q] = jnp.where(inside, 0.0, rows[k + q]) - total(
                [columns[q][m] * w[m] for m in range(8)]
            )
        mine, scale = v[0], a[0][0]
        for m in range(1, 8):
            mine = jnp.where(sub == m, v[m], mine)
            scale = jnp.where(sub == m, a[m][m], scale)
        out.append(jnp.where(lane <= base + sub, mine * lax.rsqrt(scale), 0.0))
    return jnp.concatenate(out, axis=0)


def factor_blocks(a_ref, l_ref, inv_ref, s_ref, first, last, order):
    count = order // TILE
    tri = lax.broadcasted_iota(jnp.int32, (TILE, TILE), 0) >= lax.broadcasted_iota(
        jnp.int32, (TILE, TILE), 1
    )

    def step(kb, _):
        at = pl.multiple_of(kb * TILE, TILE)
        inverse = inverse_factor(a_ref[pl.ds(at, TILE), pl.ds(at, TILE)], s_ref)
        inv_ref[pl.ds(at, TILE), pl.ds(pl.multiple_of((kb % 2) * TILE, TILE), TILE)] = inverse
        for q in range(first, last):

            @pl.when(kb == q)
            def _():
                lo = q * TILE
                half = q % 2 * TILE
                inverse = inv_ref[lo : lo + TILE, half : half + TILE]
                panel = dot_t(a_ref[lo:order, lo : lo + TILE], inverse)
                l_ref[lo : lo + TILE, lo : lo + TILE] = jnp.where(tri, panel[:TILE], 0.0)
                if q + 1 < count:
                    l_ref[lo + TILE : order, lo : lo + TILE] = panel[TILE:]
                    for j in range(q + 1, count):
                        left = panel[(j - q) * TILE :]
                        a_ref[j * TILE : order, j * TILE : (j + 1) * TILE] = a_ref[
                            j * TILE : order, j * TILE : (j + 1) * TILE
                        ] - dot_t(left, left[:TILE])
                if half:
                    up = inv_ref[lo - TILE : lo, :TILE]
                    inv_ref[lo - TILE : lo, TILE:] = jnp.zeros((TILE, TILE), jnp.float32)
                    inv_ref[lo : lo + TILE, :TILE] = -dot(
                        inverse, dot(l_ref[lo : lo + TILE, lo - TILE : lo], up)
                    )

        return 0

    lax.fori_loop(first, last, step, 0)


def solve_rows(x_ref, hi_ref, lo_ref, l_ref, inv_ref, order):
    for p in range(order // WIDE):
        lo = p * WIDE
        now = slice(lo, lo + WIDE)
        part = x_ref[:, now]
        if p:
            part = part - dot_split((hi_ref[:, :lo], lo_ref[:, :lo]), split(l_ref[now, :lo]))
        part = dot_split(split(part), split(inv_ref[now, :]))
        x_ref[:, now] = part
        hi_ref[:, now], lo_ref[:, now] = split(part)


def child_kernel(tiles_ref, front_ref, factor_ref, out_ref, a_ref, b_ref, c_ref, inv_ref, s_ref, hi_ref, lo_ref, sems):
    copy_a = pltpu.make_async_copy(front_ref.at[pl.ds(0, CP), pl.ds(0, CP)], a_ref, sems.at[0])
    copy_b = pltpu.make_async_copy(front_ref.at[pl.ds(CP, REST), pl.ds(0, CP)], b_ref, sems.at[1])
    copy_c = pltpu.make_async_copy(front_ref.at[pl.ds(CP, REST), pl.ds(CP, REST)], c_ref, sems.at[2])
    copy_a.start()
    copy_b.start()
    copy_c.start()
    copy_a.wait()
    factor_ref[0:CP, :] = jnp.zeros((CP, CP), jnp.float32)
    factor_blocks(a_ref, factor_ref, inv_ref, s_ref, 0, CP // TILE, CP)
    copy_b.wait()
    solve_rows(b_ref, hi_ref, lo_ref, factor_ref, inv_ref, CP)
    factor_ref[CP:CW, :] = b_ref[...]
    copy_c.wait()
    for first in range(0, REST, WIDE):
        rows = slice(first, first + WIDE)
        wide = first + WIDE
        update = c_ref[rows, :wide] - dot_split(
            (hi_ref[rows, :], lo_ref[rows, :]), (hi_ref[:wide, :], lo_ref[:wide, :])
        )
        for k in range(2):
            i = first // TILE + k
            for j in range(i + 1):
                part = update[k * TILE : (k + 1) * TILE, j * TILE : (j + 1) * TILE]
                out_ref[pl.ds(pair_slot[i, j], DEV, stride=SLOTS), :] = part
    meta = jnp.broadcast_to(tiles_ref[0:1, :], (DEV, TILE))
    out_ref[pl.ds(META, DEV, stride=SLOTS), :] = meta
    out_ref[pl.ds(META + 1, DEV, stride=SLOTS), :] = meta


IN_VMEM = pl.BlockSpec(memory_space=pltpu.VMEM)
ANYWHERE = pl.BlockSpec(memory_space=pl.ANY)
IN_SMEM = pl.BlockSpec(memory_space=pltpu.SMEM)
PARAMS = pltpu.CompilerParams(vmem_limit_bytes=VMEM)


def cost(us):
    return pl.CostEstimate(flops=int(us * 10**9), bytes_accessed=int(us * 10**6), transcendentals=0)


def array(rows, columns=TILE, dtype=jnp.float32):
    return jax.ShapeDtypeStruct((rows, columns), dtype)


def eliminate_child(front, tiles):
    return pl.pallas_call(
        child_kernel,
        out_shape=(array(CW, CP), array(DEV * SLOTS)),
        in_specs=[IN_VMEM, ANYWHERE],
        out_specs=(IN_VMEM, IN_VMEM),
        scratch_shapes=[
            pltpu.VMEM((CP, CP), jnp.float32),
            pltpu.VMEM((REST, CP), jnp.float32),
            pltpu.VMEM((REST, REST), jnp.float32),
            pltpu.VMEM((CP, WIDE), jnp.float32),
            pltpu.VMEM((SPREAD, TILE), jnp.float32),
            pltpu.VMEM((REST, CP), jnp.bfloat16),
            pltpu.VMEM((REST, CP), jnp.bfloat16),
            pltpu.SemaphoreType.DMA((3,)),
        ],
        compiler_params=PARAMS,
        cost_estimate=cost(40),
        name="child",
    )(tiles, front)


def sum_kernel(meta_in_ref, parent_ref, in_ref, acc_ref, corner_ref, rows_ref, places_ref, pack_ref, table_ref, sems):
    piece = DEV * SLOTS // CHUNKS
    chunk = lambda k: pltpu.make_async_copy(
        in_ref.at[pl.ds(k * piece, piece)], rows_ref.at[pl.ds(k * piece, piece)], sems.at[k]
    )
    start = pltpu.make_async_copy(parent_ref, acc_ref, sems.at[CHUNKS])
    start.start()
    for k in range(CHUNKS):
        chunk(k).start()
    ids = meta_in_ref[pl.ds(META % 8, DEV, stride=8), :].astype(jnp.int32)
    as_row = (ids // 4) * 256 + (ids % 4) * 8
    as_col = (ids // 8) * 32 + ids % 8
    lane = lax.broadcasted_iota(jnp.int32, (DEV, TILE), 1)
    places_ref[...] = jnp.where(lane < 64, as_row, pltpu.roll(as_col, 64, axis=1))
    table = pltpu.make_async_copy(places_ref, table_ref, sems.at[CHUNKS + 1])
    table.start()
    table.wait()
    start.wait()
    todo = list(pair_slot.items())

    def add_child(s, _):
        base = s * SLOTS
        row_of = [table_ref[s, i] for i in range(CT)]
        col_of = [table_ref[s, 64 + j] for j in range(CT)]
        for first in range(0, len(todo), 26):
            group = todo[first : first + 26]
            places = [row_of[i] + col_of[j] for (i, j), _ in group]
            sums = [
                acc_ref[pl.ds(place, 1), :] + rows_ref[pl.ds(base + slot, 1), :]
                for place, (_, slot) in zip(places, group)
            ]
            for place, total in zip(places, sums):
                acc_ref[pl.ds(place, 1), :] = total
        return 0

    for k in range(CHUNKS):
        chunk(k).wait()
        lax.fori_loop(k * DEV // CHUNKS, (k + 1) * DEV // CHUNKS, add_child, 0)

    for (i, j), slot in corner_slot.items():
        place = (i // 4) * 256 + (i % 4) * 8 + j
        pack_ref[slot : slot + 1, :] = acc_ref[place : place + 1, :]
    pack_ref[len(corner_slot) : 2 * HALF, :] = jnp.zeros((2 * HALF - len(corner_slot), TILE), jnp.float32)

    def send(g, _):
        pltpu.make_async_copy(
            pack_ref.at[pl.ds(pl.multiple_of((g % 2) * HALF, 8), HALF)],
            corner_ref.at[pl.ds(pl.multiple_of(g * HALF, 8), HALF)],
            sems.at[0],
        ).start()
        return 0

    lax.fori_loop(0, DEV, send, 0)
    pltpu.make_async_copy(corner_ref, corner_ref, sems.at[0]).wait()


def sum_slices(parent, arrived):
    return pl.pallas_call(
        sum_kernel,
        grid=(1,),
        out_shape=(array(DEV * 32), array(DEV * HALF)),
        in_specs=[pl.BlockSpec((DEV * 8, TILE), lambda i: (0, 0)), ANYWHERE, ANYWHERE],
        out_specs=(IN_VMEM, ANYWHERE),
        scratch_shapes=[
            pltpu.VMEM((DEV * SLOTS, TILE), jnp.float32),
            pltpu.VMEM((DEV, TILE), jnp.int32),
            pltpu.VMEM((2 * HALF, TILE), jnp.float32),
            pltpu.SMEM((DEV, TILE), jnp.int32),
            pltpu.SemaphoreType.DMA((CHUNKS + 2,)),
        ],
        compiler_params=PARAMS,
        cost_estimate=cost(15),
        name="sum_slices",
    )(arrived.reshape(DEV, SLOTS, TILE)[:, META // 8 * 8 :, :].reshape(DEV * 8, TILE), parent, arrived)


def pack_kernel(acc_ref, back_ref, block_ref, sem):
    sub = lax.broadcasted_iota(jnp.int32, (8, TILE), 0)

    def pack_device(g, _):
        r = g // 8
        c = g % 8
        base = pl.multiple_of(g * BACK, 8)
        for at, place, rows in (
            (0, r * 256 + (c % 2) * 16, 16),
            (16, c * 512, 32),
            (48, c * 512 + 256, 32),
        ):
            pltpu.make_async_copy(
                acc_ref.at[pl.ds(pl.multiple_of(place, 8), rows)],
                back_ref.at[pl.ds(pl.multiple_of(base + at, 8), rows)],
                sem,
            ).start()
        odd = (r % 2) == 1
        direct = jnp.where(sub < 4, 0, 1) + 2 * c <= r
        for k in range(4):
            lower = acc_ref[pl.ds(pl.multiple_of(g * 32 + k * 8, 8), 8), :]
            m0 = acc_ref[pl.ds(pl.multiple_of(((2 * c) * 8 + r // 2) * 32 + k * 8, 8), 8), :]
            m1 = acc_ref[pl.ds(pl.multiple_of(((2 * c + 1) * 8 + r // 2) * 32 + k * 8, 8), 8), :]
            m0 = jnp.where(odd, pltpu.roll(m0, 4, axis=0), m0)
            m1 = jnp.where(odd, m1, pltpu.roll(m1, 4, axis=0))
            upper = jnp.where(sub < 4, m0, m1)
            block_ref[pl.ds(pl.multiple_of(g * 32 + k * 8, 8), 8), :] = jnp.where(direct, lower, upper)
        return 0

    lax.fori_loop(0, DEV, pack_device, 0)
    pltpu.make_async_copy(back_ref, back_ref, sem).wait()


def pack_back(acc):
    return pl.pallas_call(
        pack_kernel,
        out_shape=(array(DEV * BACK), array(DEV * BLOCK)),
        in_specs=[IN_VMEM],
        out_specs=(ANYWHERE, IN_VMEM),
        scratch_shapes=[pltpu.SemaphoreType.DMA],
        compiler_params=PARAMS,
        cost_estimate=cost(8),
        name="pack_back",
    )(acc)


def corner_kernel(where_ref, mine_ref, other_ref, l_ref, inv_ref, a_ref, s_ref):
    even = where_ref[1] % 2 == 0

    def load(halves):
        for (i, j), slot in corner_slot.items():
            a_ref[i * TILE : (i + 1) * TILE, j * TILE : (j + 1) * TILE] = halves[slot // HALF][
                pl.ds(slot % HALF, DEV, stride=HALF), :
            ]

    @pl.when(even)
    def _():
        load((mine_ref, other_ref))

    @pl.when(jnp.logical_not(even))
    def _():
        load((other_ref, mine_ref))

    l_ref[...] = jnp.zeros((PIV, PIV), jnp.float32)
    factor_blocks(a_ref, l_ref, inv_ref, s_ref, 0, PIV // TILE, PIV)


def factor_corner(where, mine, other):
    return pl.pallas_call(
        corner_kernel,
        out_shape=(array(PIV, PIV), array(PIV, WIDE)),
        in_specs=[IN_SMEM, IN_VMEM, IN_VMEM],
        out_specs=(IN_VMEM, IN_VMEM),
        scratch_shapes=[pltpu.VMEM((PIV, PIV), jnp.float32), pltpu.VMEM((SPREAD, TILE), jnp.float32)],
        compiler_params=PARAMS,
        cost_estimate=cost(50),
        name="corner",
    )(where, mine, other)


def panel_kernel(where_ref, in_ref, other_ref, l_ref, inv_ref, out_ref, x_ref, hi_ref, lo_ref):
    r = where_ref[0]
    c = where_ref[1]
    even = c % 2 == 0
    tile = lambda slot: in_ref[pl.ds(slot, DEV, stride=BACK), :]

    def load_rows(at, other_at):
        for a in range(2):
            for j in range(8):
                cols = slice(j * TILE, (j + 1) * TILE)
                x_ref[(at + a) * TILE : (at + a + 1) * TILE, cols] = tile(a * 8 + j)
                x_ref[(other_at + a) * TILE : (other_at + a + 1) * TILE, cols] = other_ref[
                    pl.ds(a * 8 + j, DEV, stride=16), :
                ]

    @pl.when(even)
    def _():
        load_rows(0, 2)

    @pl.when(jnp.logical_not(even))
    def _():
        load_rows(2, 0)

    @pl.when(r >= 2)
    def _():
        for a in range(8):
            for j in range(8):
                x_ref[PANEL + a * TILE : PANEL + (a + 1) * TILE, j * TILE : (j + 1) * TILE] = tile(16 + a * 8 + j)
        solve_rows(x_ref, hi_ref, lo_ref, l_ref, inv_ref, PIV)

    @pl.when((r >= 2) & (c >= 1))
    def _():
        out_ref[...] = dot_split(
            (hi_ref[:PANEL, :], lo_ref[:PANEL, :]), (hi_ref[PANEL:, :], lo_ref[PANEL:, :])
        )

    @pl.when((r >= 2) & (c == 0))
    def _():
        out_ref[...] = x_ref[:PANEL, :]

    @pl.when((r < 2) & (c == 0))
    def _():
        out_ref[...] = l_ref[pl.ds(pl.multiple_of(r * PANEL, PANEL), PANEL), :]

    @pl.when((r < 2) & (c >= 1))
    def _():
        out_ref[...] = jnp.zeros((PANEL, PIV), jnp.float32)


def solve_panel(where, arrived, other, corner, inverses):
    rows = 3 * PANEL
    return pl.pallas_call(
        panel_kernel,
        out_shape=array(PANEL, PIV),
        in_specs=[IN_SMEM] + [IN_VMEM] * 4,
        out_specs=IN_VMEM,
        scratch_shapes=[
            pltpu.VMEM((rows, PIV), jnp.float32),
            pltpu.VMEM((rows, PIV), jnp.bfloat16),
            pltpu.VMEM((rows, PIV), jnp.bfloat16),
        ],
        compiler_params=PARAMS,
        cost_estimate=cost(20),
        name="panel",
    )(where, arrived, other, corner, inverses)


def finish_kernel(where_ref, part_ref, in_ref, out_ref):
    r = where_ref[0]
    c = where_ref[1]
    trailing = (r >= 2) & (c >= 1)
    tile = lambda slot: in_ref[pl.ds(slot, DEV, stride=BLOCK), :]

    @pl.when(jnp.logical_not(trailing))
    def _():
        out_ref[...] = part_ref[...]

    @pl.when(trailing)
    def _():
        for q in range(2):
            for a in range(4):
                for b in range(4):
                    spot = (
                        slice(a * TILE, (a + 1) * TILE),
                        slice(q * PANEL + b * TILE, q * PANEL + (b + 1) * TILE),
                    )
                    mirrored = (r < 2 * c + q) | ((r == 2 * c + q) & (a < b))

                    @pl.when(mirrored)
                    def _():
                        out_ref[spot] = tile(b * 8 + q * 4 + a).T - part_ref[spot]

                    @pl.when(jnp.logical_not(mirrored))
                    def _():
                        out_ref[spot] = tile(a * 8 + q * 4 + b) - part_ref[spot]


def finish(where, part, arrived):
    return pl.pallas_call(
        finish_kernel,
        out_shape=array(PANEL, PIV),
        in_specs=[IN_SMEM, IN_VMEM, IN_VMEM],
        out_specs=IN_VMEM,
        compiler_params=pltpu.CompilerParams(vmem_limit_bytes=16 * 1024 * 1024),
        cost_estimate=cost(6),
        name="finish",
    )(where, part, arrived)


def exchange(x):
    y = x.reshape(DEV, x.shape[0] // DEV, TILE)
    return lax.all_to_all(y, AXES, 0, 0, tiled=True).reshape(x.shape)


def swap_cores(x):
    return lax.ppermute(x, "col", [(d, d ^ 1) for d in range(8)])


def on_device(child_fronts, child_tiles, parent_front):
    row = lax.axis_index("row")
    col = lax.axis_index("col")
    parent = parent_front.reshape(4, TILE, 8, TILE).transpose(1, 0, 2, 3).reshape(DEV * 32, TILE)
    parent = exchange(parent)
    tiles = jnp.pad(child_tiles.astype(jnp.float32), ((0, 7), (0, TILE - CT)))
    factor, outgoing = eliminate_child(child_fronts[0], tiles)
    outgoing, parent = lax.optimization_barrier((outgoing, parent))
    acc, corner_rows = sum_slices(parent, exchange(outgoing))
    where = jnp.stack([row, col]).astype(jnp.int32)
    panel_rows, block_rows = pack_back(acc)
    mine, panel_rows, block_rows = lax.optimization_barrier(
        (exchange(corner_rows), panel_rows, block_rows)
    )
    other = swap_cores(mine)
    corner, inverses = factor_corner(where, mine, other)
    arrived, corner, inverses = lax.optimization_barrier((exchange(panel_rows), corner, inverses))
    shared = arrived.reshape(DEV, BACK, TILE)[:, :16, :].reshape(DEV * 16, TILE)
    block_rows, arrived = lax.optimization_barrier((block_rows, arrived))
    part = solve_panel(where, arrived, swap_cores(shared), corner, inverses)
    result = finish(where, part, exchange(block_rows))
    return factor[None], result


def solution(mesh):
    placed = (P(AXES, None, None), P(AXES, None), P("row", "col"))
    return jax.shard_map(
        on_device,
        mesh=mesh,
        in_specs=placed,
        out_specs=(P(AXES, None, None), P("row", "col")),
        check_vma=False,
    )
```

time: 355 us -> 288 us (0.81)
  the two profiles are of different devices: /device:TPU:26 before, /device:TPU:1 now
where the time goes in v2:
time: 288 us; the launch traced here: 282 us
  Pallas kernels  104 us (36%)
  blocking collectives  73.5 us (26%)
  waiting for transfers between devices  64.4 us (22%)
  starting transfers between devices  27.2 us (9%)
  local copies, waits for them, and re-layouts  11.1 us (4%)
    all_to_all x1, blocking collectives, exchange(): return lax.all_to_all(y, AXES, 0, 0, tiled=True).reshape(x.shape)  73.5 us
    all_to_all x4, waiting for transfers between devices, exchange(): return lax.all_to_all(y, AXES, 0, 0, tiled=True).reshape(x.shape)  64.4 us
    pallas_call x1, Pallas kernels, factor_corner(): pl.pallas_call(corner_kernel, out_shape=(array(PIV, PIV), array(PIV, WIDE...  40 us
    pallas_call x1, Pallas kernels, eliminate_child(): pl.pallas_call(child_kernel, out_shape=(array(CW, CP), array(DEV * SLOTS)...  29.3 us
    all_to_all x4, starting transfers between devices, exchange(): return lax.all_to_all(y, AXES, 0, 0, tiled=True).reshape(x.shape)  25.1 us
    pallas_call x1, Pallas kernels, sum_slices(): pl.pallas_call(sum_kernel, grid=(1,), out_shape=(array(DEV * 32), array(D...  19.2 us
    pallas_call x1, Pallas kernels, pack_back(): pl.pallas_call(pack_kernel, out_shape=(array(DEV * BACK), array(DEV * BLO...  6.94 us
    pallas_call x1, Pallas kernels, solve_panel(): pl.pallas_call(panel_kernel, out_shape=array(PANEL, PIV), in_specs=[IN_SM...  6.9 us
  transfers between devices with their start and end apart: 6, of which 4 were waited for; matrix products, arithmetic and copies ran while one was open for 0% of the time, Pallas kernels for 29%

profile of v2, /device:TPU:1, one launch (start us, length us, event | category | flops | bytes accessed | tf_op | source)
XLA Modules:
  0.0 282.4 jit_solution(13264715731885607478)
XLA Ops:
  0.6 2.1 copy.6
  2.7 1.6 copy_bitcast_fusion
  4.3 0.0 copy-start.6
  4.3 11.5 %all-to-all-start = ((f32[128,32,128]{2,1,0:T(8,128)}), f32[128,32,128]{2,1,0:T(8,128)S(1)}, u32[]{:S(2)}, u32[]{:S(2)}) async-start(f32[128,32,128]{2,1,0:T(8,128)} %copy_bitcast_fusion), calls=%async_computation | async-start | bytes 4194304 | tf_op jit(solution)/shard_map/all_to_all | solution.py:512
  15.8 0.0 copy-done.6
  15.8 0.6 pad.4.tiles_ref
  16.4 29.3 %child.1 = (f32[2048,512]{1,0:T(8,128)}, f32[10240,128]{1,0:T(8,128)}) custom-call(f32[8,128]{1,0:T(8,128)} %pad.4.tiles_ref, f32[2048,2048]{1,0:T(8,128)} %bitcast.41), custom_call_target="tpu_custom_call" | custom-call | flops 40000000000 | bytes 40000000 | tf_op jit(solution)/shard_map/child/pallas_call | solution.py:224
  45.8 0.5 all-to-all-done
  46.3 0.0 copy-start.3
  46.3 73.5 %all_to_all.25 = f32[128,80,128]{2,1,0:T(8,128)S(1)} all-to-all(f32[128,80,128]{2,1,0:T(8,128)} %bitcast.33), channel_id=1, replica_groups=mesh['row'=16,'col'=8] {'row','col'}, dimensions={0} | all-to-all | bytes 10485760 | tf_op jit(solution)/shard_map/all_to_all | solution.py:512
  119.9 0.0 copy-done.3
  119.9 0.0 copy-start.2
  119.9 0.9 slice_bitcast_fusion.meta_in_ref
  120.8 1.6 copy-done.2
  122.3 19.2 %sum_slices.1 = (f32[4096,128]{1,0:T(8,128)}, f32[3072,128]{1,0:T(8,128)}) custom-call(f32[1024,128]{1,0:T(8,128)} %slice_bitcast_fusion.meta_in_ref, f32[4096,128]{1,0:T(8,128)} %bitcast.36, f32[10240,128]{1,0:T(8,128)} %bitcast.31), custom_call_target="tpu_custom_call" | custom-call | flops 15000000512 | bytes 15000000 | tf_op jit(solution)/shard_map/sum_slices/pallas_call | solution.py:302
  141.6 4.3 %all-to-all-start.2 = ((f32[128,24,128]{2,1,0:T(8,128)}), f32[128,24,128]{2,1,0:T(8,128)S(1)}, u32[]{:S(2)}, u32[]{:S(2)}) async-start(f32[128,24,128]{2,1,0:T(8,128)} %bitcast.39), calls=%async_computation.2 | async-start | bytes 3145728 | tf_op jit(solution)/shard_map/all_to_all | solution.py:512
  145.9 6.9 %pack_back.1 = (f32[10240,128]{1,0:T(8,128)}, f32[4096,128]{1,0:T(8,128)}) custom-call(f32[4096,128]{1,0:T(8,128)} %get-tuple-element.25.acc_ref), custom_call_target="tpu_custom_call" | custom-call | flops 8000000000 | bytes 8000000 | tf_op jit(solution)/shard_map/pack_back/pallas_call | solution.py:355
  152.9 18.1 %all-to-all-done.2 = f32[128,24,128]{2,1,0:T(8,128)S(1)} async-done(((f32[128,24,128]{2,1,0:T(8,128)}), f32[128,24,128]{2,1,0:T(8,128)S(1)}, u32[]{:S(2)}, u32[]{:S(2)}) %all-to-all-start.2) | async-done | bytes 1572896 | tf_op jit(solution)/shard_map/all_to_all | solution.py:512
  171.0 0.0 copy-start.4
  171.0 0.9 collective-permute-start
  171.9 0.2 copy-done.4
  172.1 5.4 %all-to-all-start.3 = ((f32[128,80,128]{2,1,0:T(8,128)}), f32[128,80,128]{2,1,0:T(8,128)}, u32[]{:S(2)}, u32[]{:S(2)}) async-start(f32[128,80,128]{2,1,0:T(8,128)} %bitcast.32), calls=%async_computation.3 | async-start | bytes 10485760 | tf_op jit(solution)/shard_map/all_to_all | solution.py:512
  177.6 0.7 pad_add_fusion.where_ref
  178.2 0.0 collective-permute-done.other_ref
  178.2 0.0 copy-start.5
  178.2 1.2 copy-done.5
  179.4 40.0 %corner.1 = (f32[1024,1024]{1,0:T(8,128)}, f32[1024,256]{1,0:T(8,128)}) custom-call(s32[2]{0:T(128)} %pad_add_fusion.where_ref, f32[3072,128]{1,0:T(8,128)} %bitcast.38, f32[3072,128]{1,0:T(8,128)} %copy-done.5), custom_call_target="tpu_custom_call" | custom-call | flops 49999998976 | bytes 50000000 | tf_op jit(solution)/shard_map/corner/pallas_call | solution.py:389
  219.4 22.1 %all-to-all-done.3 = f32[128,80,128]{2,1,0:T(8,128)} async-done(((f32[128,80,128]{2,1,0:T(8,128)}), f32[128,80,128]{2,1,0:T(8,128)}, u32[]{:S(2)}, u32[]{:S(2)}) %all-to-all-start.3) | async-done | bytes 5242912 | tf_op jit(solution)/shard_map/all_to_all | solution.py:512
  241.5 1.3 slice.9
  242.8 1.2 collective-permute-start.1
  244.0 3.8 %all-to-all-start.4 = ((f32[128,32,128]{2,1,0:T(8,128)}), f32[128,32,128]{2,1,0:T(8,128)S(1)}, u32[]{:S(2)}, u32[]{:S(2)}) async-start(f32[128,32,128]{2,1,0:T(8,128)} %bitcast.35), calls=%async_computation.4 | async-start | bytes 4194304 | tf_op jit(solution)/shard_map/all_to_all | solution.py:512
  247.8 0.0 copy-start
  247.8 0.0 collective-permute-done.1.other_ref
  247.8 6.9 %panel.1.part_ref = f32[512,1024]{1,0:T(8,128)} custom-call(s32[2]{0:T(128)} %pad_add_fusion.where_ref, f32[10240,128]{1,0:T(8,128)} %bitcast.13.in_ref, f32[2048,128]{1,0:T(8,128)} %collective-permute-done.1.other_ref, f32[1024,1024]{1,0:T(8,128)} %get-tuple-element.35.l_ref, f32[1024,256]{1,0:T(8,128)} %get-tuple-element.36.inv_ref), custom_call_target="tpu_custom_call" | custom-call | flops 20000000000 | bytes 20000000 | tf_op jit(solution)/shard_map/panel/pallas_call | solution.py:452
  254.7 23.6 %all-to-all-done.4 = f32[128,32,128]{2,1,0:T(8,128)S(1)} async-done(((f32[128,32,128]{2,1,0:T(8,128)}), f32[128,32,128]{2,1,0:T(8,128)S(1)}, u32[]{:S(2)}, u32[]{:S(2)}) %all-to-all-start.4) | async-done | bytes 2097184 | tf_op jit(solution)/shard_map/all_to_all | solution.py:512
  278.3 0.0 copy-done
  278.3 0.0 copy-start.1
  278.3 1.6 copy-done.1
  279.9 2.0 finish.1
  (1 shorter events, 0.0 us)
Async XLA Ops:
  4.3 11.5 %copy-start.6 = (s32[1,12]{1,0:T(1,128)S(1)}, s32[1,12]{1,0:T(1,128)}, u32[]{:S(2)}) copy-start(s32[1,12]{1,0:T(1,128)} %param.4) | copy-start | bytes 148
  4.3 42.0 %all-to-all-start = ((f32[128,32,128]{2,1,0:T(8,128)}), f32[128,32,128]{2,1,0:T(8,128)S(1)}, u32[]{:S(2)}, u32[]{:S(2)}) async-start(f32[128,32,128]{2,1,0:T(8,128)} %copy_bitcast_fusion), calls=%async_computation | async-start | bytes 4194304 | tf_op jit(solution)/shard_map/all_to_all | solution.py:512
  46.3 73.5 %copy-start.3 = (f32[128,32,128]{2,1,0:T(8,128)}, f32[128,32,128]{2,1,0:T(8,128)S(1)}, u32[]{:S(2)}) copy-start(f32[128,32,128]{2,1,0:T(8,128)S(1)} %all-to-all-done) | copy-start | bytes 6291460
  119.9 2.5 copy-start.2
  141.6 29.4 %all-to-all-start.2 = ((f32[128,24,128]{2,1,0:T(8,128)}), f32[128,24,128]{2,1,0:T(8,128)S(1)}, u32[]{:S(2)}, u32[]{:S(2)}) async-start(f32[128,24,128]{2,1,0:T(8,128)} %bitcast.39), calls=%async_computation.2 | async-start | bytes 3145728 | tf_op jit(solution)/shard_map/all_to_all | solution.py:512
  171.0 1.2 copy-start.4
  171.0 7.3 %collective-permute-start = (f32[3072,128]{1,0:T(8,128)S(1)}, f32[3072,128]{1,0:T(8,128)S(1)}, u32[]{:S(2)}, u32[]{:S(2)}) collective-permute-start(f32[3072,128]{1,0:T(8,128)S(1)} %bitcast.37), channel_id=1, source_target_pairs={{0,1},{1,0},{2,3},{3,2},{4,5},{5,4},{6,7},{7,6},{8,9},{9,8},{10,11... | collective-permute-start | bytes 4718600 | tf_op jit(solution)/shard_map/ppermute | solution.py:516
  172.1 69.3 %all-to-all-start.3 = ((f32[128,80,128]{2,1,0:T(8,128)}), f32[128,80,128]{2,1,0:T(8,128)}, u32[]{:S(2)}, u32[]{:S(2)}) async-start(f32[128,80,128]{2,1,0:T(8,128)} %bitcast.32), calls=%async_computation.3 | async-start | bytes 10485760 | tf_op jit(solution)/shard_map/all_to_all | solution.py:512
  178.2 1.2 copy-start.5
  242.8 5.0 %collective-permute-start.1 = (f32[2048,128]{1,0:T(8,128)S(1)}, f32[2048,128]{1,0:T(8,128)}, u32[]{:S(2)}, u32[]{:S(2)}) collective-permute-start(f32[2048,128]{1,0:T(8,128)S(1)} %bitcast.40), channel_id=1, source_target_pairs={{0,1},{1,0},{2,3},{3,2},{4,5},{5,4},{6,7},{7,6},{8,9},{9,8},{10,11... | collective-permute-start | bytes 3145736 | tf_op jit(solution)/shard_map/ppermute | solution.py:516
  244.0 34.4 %all-to-all-start.4 = ((f32[128,32,128]{2,1,0:T(8,128)}), f32[128,32,128]{2,1,0:T(8,128)S(1)}, u32[]{:S(2)}, u32[]{:S(2)}) async-start(f32[128,32,128]{2,1,0:T(8,128)} %bitcast.35), calls=%async_computation.4 | async-start | bytes 4194304 | tf_op jit(solution)/shard_map/all_to_all | solution.py:512
  247.8 30.6 %copy-start = (s32[2]{0:T(128)S(1)}, s32[2]{0:T(128)}, u32[]{:S(2)}) copy-start(s32[2]{0:T(128)} %pad_add_fusion.where_ref) | copy-start | bytes 28
  278.3 1.6 copy-start.1

commit v3 on v2

--- a/solution.py
+++ b/solution.py
@@ -18,7 +18,7 @@
 PAIRS = CT * (CT + 1) // 2
 AXES = ("row", "col")
 PRECISE = lax.Precision.HIGHEST
-VMEM = 56 * 1024 * 1024
+VMEM = 61 * 1024 * 1024
 
 SLOTS = 80
 META = PAIRS
@@ -176,20 +176,34 @@
         hi_ref[:, now], lo_ref[:, now] = split(part)
 
 
-def child_kernel(tiles_ref, front_ref, factor_ref, out_ref, a_ref, b_ref, c_ref, inv_ref, s_ref, hi_ref, lo_ref, sems):
+def child_kernel(
+    tiles_ref, front_ref, factor_out, rows_out,
+    a_ref, b_ref, c_ref, inv_ref, s_ref, hi_ref, lo_ref, factor_ref, rows_ref, sems,
+):
     copy_a = pltpu.make_async_copy(front_ref.at[pl.ds(0, CP), pl.ds(0, CP)], a_ref, sems.at[0])
     copy_b = pltpu.make_async_copy(front_ref.at[pl.ds(CP, REST), pl.ds(0, CP)], b_ref, sems.at[1])
     copy_c = pltpu.make_async_copy(front_ref.at[pl.ds(CP, REST), pl.ds(CP, REST)], c_ref, sems.at[2])
     copy_a.start()
     copy_b.start()
     copy_c.start()
+    flat_ref = rows_ref.reshape(DEV * SLOTS, TILE)
+    lane = lax.broadcasted_iota(jnp.int32, (DEV, TILE), 1)
+    meta = jnp.zeros((DEV, TILE), jnp.int32)
+    for t in range(CT):
+        meta = jnp.where(lane == t, tiles_ref[0, t], meta)
+    flat_ref[pl.ds(META, DEV, stride=SLOTS), :] = meta.astype(jnp.float32)
+    flat_ref[pl.ds(META + 1, DEV, stride=SLOTS), :] = jnp.zeros((DEV, TILE), jnp.float32)
+    factor_ref[...] = jnp.zeros((CP, CP), jnp.float32)
     copy_a.wait()
-    factor_ref[0:CP, :] = jnp.zeros((CP, CP), jnp.float32)
     factor_blocks(a_ref, factor_ref, inv_ref, s_ref, 0, CP // TILE, CP)
+    send_corner = pltpu.make_async_copy(factor_ref, factor_out.at[pl.ds(0, CP)], sems.at[3])
+    send_corner.start()
     copy_b.wait()
     solve_rows(b_ref, hi_ref, lo_ref, factor_ref, inv_ref, CP)
-    factor_ref[CP:CW, :] = b_ref[...]
+    send_below = pltpu.make_async_copy(b_ref, factor_out.at[pl.ds(CP, REST)], sems.at[4])
+    send_below.start()
     copy_c.wait()
+    sends = []
     for first in range(0, REST, WIDE):
         rows = slice(first, first + WIDE)
         wide = first + WIDE
@@ -200,10 +214,21 @@
             i = first // TILE + k
             for j in range(i + 1):
                 part = update[k * TILE : (k + 1) * TILE, j * TILE : (j + 1) * TILE]
-                out_ref[pl.ds(pair_slot[i, j], DEV, stride=SLOTS), :] = part
-    meta = jnp.broadcast_to(tiles_ref[0:1, :], (DEV, TILE))
-    out_ref[pl.ds(META, DEV, stride=SLOTS), :] = meta
-    out_ref[pl.ds(META + 1, DEV, stride=SLOTS), :] = meta
+                flat_ref[pl.ds(pair_slot[i, j], DEV, stride=SLOTS), :] = part
+        done = SLOTS if wide == REST else (pair_slot[i, i] + 1) // 8 * 8
+        sent = 8 * sum(groups for groups, _ in sends)
+        if done > sent:
+            copy = pltpu.make_async_copy(
+                rows_ref.at[:, pl.ds(sent, done - sent)],
+                rows_out.at[:, pl.ds(sent, done - sent)],
+                sems.at[5 + len(sends)],
+            )
+            copy.start()
+            sends.append(((done - sent) // 8, copy))
+    send_corner.wait()
+    send_below.wait()
+    for _, copy in sends:
+        copy.wait()
 
 
 IN_VMEM = pl.BlockSpec(memory_space=pltpu.VMEM)
@@ -221,11 +246,11 @@
 
 
 def eliminate_child(front, tiles):
-    return pl.pallas_call(
+    factor, rows = pl.pallas_call(
         child_kernel,
-        out_shape=(array(CW, CP), array(DEV * SLOTS)),
-        in_specs=[IN_VMEM, ANYWHERE],
-        out_specs=(IN_VMEM, IN_VMEM),
+        out_shape=(array(CW, CP), jax.ShapeDtypeStruct((DEV, SLOTS, TILE), jnp.float32)),
+        in_specs=[IN_SMEM, ANYWHERE],
+        out_specs=(ANYWHERE, ANYWHERE),
         scratch_shapes=[
             pltpu.VMEM((CP, CP), jnp.float32),
             pltpu.VMEM((REST, CP), jnp.float32),
@@ -234,15 +259,18 @@
             pltpu.VMEM((SPREAD, TILE), jnp.float32),
             pltpu.VMEM((REST, CP), jnp.bfloat16),
             pltpu.VMEM((REST, CP), jnp.bfloat16),
-            pltpu.SemaphoreType.DMA((3,)),
+            pltpu.VMEM((CP, CP), jnp.float32),
+            pltpu.VMEM((DEV, SLOTS, TILE), jnp.float32),
+            pltpu.SemaphoreType.DMA((5 + REST // WIDE,)),
         ],
         compiler_params=PARAMS,
         cost_estimate=cost(40),
         name="child",
     )(tiles, front)
-
-
-def sum_kernel(meta_in_ref, parent_ref, in_ref, acc_ref, corner_ref, rows_ref, places_ref, pack_ref, table_ref, sems):
+    return factor, rows.reshape(DEV * SLOTS, TILE)
+
+
+def sum_kernel(meta_in_ref, parent_ref, in_ref, acc_ref, corner_ref, rows_ref, half_ref, places_ref, pack_ref, table_ref, sems):
     piece = DEV * SLOTS // CHUNKS
     chunk = lambda k: pltpu.make_async_copy(
         in_ref.at[pl.ds(k * piece, piece)], rows_ref.at[pl.ds(k * piece, piece)], sems.at[k]
@@ -251,7 +279,8 @@
     start.start()
     for k in range(CHUNKS):
         chunk(k).start()
-    ids = meta_in_ref[pl.ds(META % 8, DEV, stride=8), :].astype(jnp.int32)
+    ids = meta_in_ref.reshape(DEV * 8, TILE)[pl.ds(META % 8, DEV, stride=8), :].astype(jnp.int32)
+    half_ref[...] = jnp.zeros((DEV * 32, TILE), jnp.float32)
     as_row = (ids // 4) * 256 + (ids % 4) * 8
     as_col = (ids // 8) * 32 + ids % 8
     lane = lax.broadcasted_iota(jnp.int32, (DEV, TILE), 1)
@@ -262,25 +291,28 @@
     start.wait()
     todo = list(pair_slot.items())
 
-    def add_child(s, _):
-        base = s * SLOTS
-        row_of = [table_ref[s, i] for i in range(CT)]
-        col_of = [table_ref[s, 64 + j] for j in range(CT)]
-        for first in range(0, len(todo), 26):
-            group = todo[first : first + 26]
-            places = [row_of[i] + col_of[j] for (i, j), _ in group]
-            sums = [
-                acc_ref[pl.ds(place, 1), :] + rows_ref[pl.ds(base + slot, 1), :]
-                for place, (_, slot) in zip(places, group)
-            ]
-            for place, total in zip(places, sums):
-                acc_ref[pl.ds(place, 1), :] = total
+    def add_children(p, _):
+        pair = []
+        for s, to_ref in ((2 * p, acc_ref), (2 * p + 1, half_ref)):
+            row_of = [table_ref[s, i] for i in range(CT)]
+            col_of = [table_ref[s, 64 + j] for j in range(CT)]
+            pair.append((s * SLOTS, to_ref, row_of, col_of))
+        for first in range(0, len(todo), 13):
+            sums = []
+            for base, to_ref, row_of, col_of in pair:
+                for (i, j), slot in todo[first : first + 13]:
+                    place = row_of[i] + col_of[j]
+                    value = to_ref[pl.ds(place, 1), :] + rows_ref[pl.ds(base + slot, 1), :]
+                    sums.append((to_ref, place, value))
+            for to_ref, place, value in sums:
+                to_ref[pl.ds(place, 1), :] = value
         return 0
 
     for k in range(CHUNKS):
         chunk(k).wait()
-        lax.fori_loop(k * DEV // CHUNKS, (k + 1) * DEV // CHUNKS, add_child, 0)
-
+        lax.fori_loop(k * DEV // CHUNKS // 2, (k + 1) * DEV // CHUNKS // 2, add_children, 0)
+
+    acc_ref[...] = acc_ref[...] + half_ref[...]
     for (i, j), slot in corner_slot.items():
         place = (i // 4) * 256 + (i % 4) * 8 + j
         pack_ref[slot : slot + 1, :] = acc_ref[place : place + 1, :]
@@ -303,10 +335,11 @@
         sum_kernel,
         grid=(1,),
         out_shape=(array(DEV * 32), array(DEV * HALF)),
-        in_specs=[pl.BlockSpec((DEV * 8, TILE), lambda i: (0, 0)), ANYWHERE, ANYWHERE],
+        in_specs=[pl.BlockSpec((DEV, 8, TILE), lambda i: (0, META // 8, 0)), ANYWHERE, ANYWHERE],
         out_specs=(IN_VMEM, ANYWHERE),
         scratch_shapes=[
             pltpu.VMEM((DEV * SLOTS, TILE), jnp.float32),
+            pltpu.VMEM((DEV * 32, TILE), jnp.float32),
             pltpu.VMEM((DEV, TILE), jnp.int32),
             pltpu.VMEM((2 * HALF, TILE), jnp.float32),
             pltpu.SMEM((DEV, TILE), jnp.int32),
@@ -315,7 +348,7 @@
         compiler_params=PARAMS,
         cost_estimate=cost(15),
         name="sum_slices",
-    )(arrived.reshape(DEV, SLOTS, TILE)[:, META // 8 * 8 :, :].reshape(DEV * 8, TILE), parent, arrived)
+    )(arrived.reshape(DEV, SLOTS, TILE), parent, arrived)
 
 
 def pack_kernel(acc_ref, back_ref, block_ref, sem):
@@ -501,7 +534,7 @@
         out_shape=array(PANEL, PIV),
         in_specs=[IN_SMEM, IN_VMEM, IN_VMEM],
         out_specs=IN_VMEM,
-        compiler_params=pltpu.CompilerParams(vmem_limit_bytes=16 * 1024 * 1024),
+        compiler_params=PARAMS,
         cost_estimate=cost(6),
         name="finish",
     )(where, part, arrived)
@@ -521,8 +554,7 @@
     col = lax.axis_index("col")
     parent = parent_front.reshape(4, TILE, 8, TILE).transpose(1, 0, 2, 3).reshape(DEV * 32, TILE)
     parent = exchange(parent)
-    tiles = jnp.pad(child_tiles.astype(jnp.float32), ((0, 7), (0, TILE - CT)))
-    factor, outgoing = eliminate_child(child_fronts[0], tiles)
+    factor, outgoing = eliminate_child(child_fronts[0], child_tiles)
     outgoing, parent = lax.optimization_barrier((outgoing, parent))
     acc, corner_rows = sum_slices(parent, exchange(outgoing))
     where = jnp.stack([row, col]).astype(jnp.int32)

time: 288 us -> 284 us (0.986)
  local copies, waits for them, and re-layouts: 11.1 us -> 7.57 us
    unnamed x15 -> x7, local copies, waits for them, and re-layouts: 6.64 us -> 3.63 us
  transfers between devices with their start and end apart: 6 -> 6, of which waited for: 4 -> 4; matrix products, arithmetic and copies ran while one was open for 0% -> 0% of each run, Pallas kernels for 29% -> 30%
where the time goes in v3:
time: 284 us; the launch traced here: 278 us
  Pallas kernels  103 us (36%)
  blocking collectives  72.2 us (25%)
  waiting for transfers between devices  67.1 us (24%)
  starting transfers between devices  27.1 us (10%)
  local copies, waits for them, and re-layouts  7.57 us (3%)
    all_to_all x1, blocking collectives, exchange(): return lax.all_to_all(y, AXES, 0, 0, tiled=True).reshape(x.shape)  72.2 us
    all_to_all x4, waiting for transfers between devices, exchange(): return lax.all_to_all(y, AXES, 0, 0, tiled=True).reshape(x.shape)  67.1 us
    pallas_call x1, Pallas kernels, factor_corner(): pl.pallas_call(corner_kernel, out_shape=(array(PIV, PIV), array(PIV, WIDE...  39.9 us
    pallas_call x1, Pallas kernels, eliminate_child(): pl.pallas_call(child_kernel, out_shape=(array(CW, CP), jax.ShapeDtypeStru...  28.5 us
    all_to_all x4, starting transfers between devices, exchange(): return lax.all_to_all(y, AXES, 0, 0, tiled=True).reshape(x.shape)  24.8 us
    pallas_call x1, Pallas kernels, sum_slices(): pl.pallas_call(sum_kernel, grid=(1,), out_shape=(array(DEV * 32), array(D...  16.8 us
    pallas_call x1, Pallas kernels, pack_back(): pl.pallas_call(pack_kernel, out_shape=(array(DEV * BACK), array(DEV * BLO...  6.94 us
    pallas_call x1, Pallas kernels, solve_panel(): pl.pallas_call(panel_kernel, out_shape=array(PANEL, PIV), in_specs=[IN_SM...  6.93 us
  transfers between devices with their start and end apart: 6, of which 4 were waited for; matrix products, arithmetic and copies ran while one was open for 0% of the time, Pallas kernels for 30%

profile of v3, /device:TPU:1, one launch (start us, length us, event | category | flops | bytes accessed | tf_op | source)
XLA Modules:
  0.0 278.4 jit_solution(985915740400647571)
XLA Ops:
  0.6 2.1 copy.6
  2.7 1.6 copy_bitcast_fusion
  4.3 11.5 %all-to-all-start = ((f32[128,32,128]{2,1,0:T(8,128)}), f32[128,32,128]{2,1,0:T(8,128)S(1)}, u32[]{:S(2)}, u32[]{:S(2)}) async-start(f32[128,32,128]{2,1,0:T(8,128)} %copy_bitcast_fusion), calls=%async_computation | async-start | bytes 4194304 | tf_op jit(solution)/shard_map/all_to_all | solution.py:545
  15.8 28.5 %child.1 = (f32[2048,512]{1,0:T(8,128)}, f32[128,80,128]{2,1,0:T(8,128)}) custom-call(s32[1,12]{1,0:T(1,128)} %tiles_ref.1, f32[2048,2048]{1,0:T(8,128)} %bitcast.37), custom_call_target="tpu_custom_call" | custom-call | flops 40000000000 | bytes 40000000 | tf_op jit(solution)/shard_map/child/pallas_call | solution.py:249
  44.3 2.0 all-to-all-done
  46.3 0.0 copy-start.1
  46.3 72.2 %all_to_all.25.meta_in_ref = f32[128,80,128]{2,1,0:T(8,128)} all-to-all(f32[128,80,128]{2,1,0:T(8,128)} %get-tuple-element.21), channel_id=1, replica_groups=mesh['row'=16,'col'=8] {'row','col'}, dimensions={0} | all-to-all | bytes 10485760 | tf_op jit(solution)/shard_map/all_to_all | solution.py:545
  118.5 0.0 copy-done.1
  118.5 16.8 %sum_slices.1 = (f32[4096,128]{1,0:T(8,128)}, f32[3072,128]{1,0:T(8,128)}) custom-call(f32[128,80,128]{2,1,0:T(8,128)} %all_to_all.25.meta_in_ref, f32[4096,128]{1,0:T(8,128)} %bitcast.33, f32[10240,128]{1,0:T(8,128)} %bitcast.30), custom_call_target="tpu_custom_call" | custom-call | flops 15000000512 | bytes 15000000 | tf_op jit(solution)/shard_map/sum_slices/pallas_call | solution.py:334
  135.3 4.3 %all-to-all-start.2 = ((f32[128,24,128]{2,1,0:T(8,128)}), f32[128,24,128]{2,1,0:T(8,128)S(1)}, u32[]{:S(2)}, u32[]{:S(2)}) async-start(f32[128,24,128]{2,1,0:T(8,128)} %bitcast.36), calls=%async_computation.2 | async-start | bytes 3145728 | tf_op jit(solution)/shard_map/all_to_all | solution.py:545
  139.7 6.9 %pack_back.1 = (f32[10240,128]{1,0:T(8,128)}, f32[4096,128]{1,0:T(8,128)}) custom-call(f32[4096,128]{1,0:T(8,128)} %get-tuple-element.25.acc_ref), custom_call_target="tpu_custom_call" | custom-call | flops 8000000000 | bytes 8000000 | tf_op jit(solution)/shard_map/pack_back/pallas_call | solution.py:388
  146.6 18.1 %all-to-all-done.2 = f32[128,24,128]{2,1,0:T(8,128)S(1)} async-done(((f32[128,24,128]{2,1,0:T(8,128)}), f32[128,24,128]{2,1,0:T(8,128)S(1)}, u32[]{:S(2)}, u32[]{:S(2)}) %all-to-all-start.2) | async-done | bytes 1572896 | tf_op jit(solution)/shard_map/all_to_all | solution.py:545
  164.7 0.0 copy-start.2
  164.7 0.9 collective-permute-start
  165.6 0.2 copy-done.2
  165.9 5.4 %all-to-all-start.3 = ((f32[128,80,128]{2,1,0:T(8,128)}), f32[128,80,128]{2,1,0:T(8,128)}, u32[]{:S(2)}, u32[]{:S(2)}) async-start(f32[128,80,128]{2,1,0:T(8,128)} %bitcast.29), calls=%async_computation.3 | async-start | bytes 10485760 | tf_op jit(solution)/shard_map/all_to_all | solution.py:545
  171.3 0.6 pad_add_fusion.where_ref
  171.9 0.0 collective-permute-done.other_ref
  171.9 39.9 %corner.1 = (f32[1024,1024]{1,0:T(8,128)}, f32[1024,256]{1,0:T(8,128)}) custom-call(s32[2]{0:T(128)} %pad_add_fusion.where_ref, f32[3072,128]{1,0:T(8,128)} %bitcast.35, f32[3072,128]{1,0:T(8,128)} %collective-permute-done.other_ref), custom_call_target="tpu_custom_call" | custom-call | flops 49999998976 | bytes 50000000 | tf_op jit(solution)/shard_map/corner/pallas_call | solution.py:422
  211.8 23.4 %all-to-all-done.3 = f32[128,80,128]{2,1,0:T(8,128)} async-done(((f32[128,80,128]{2,1,0:T(8,128)}), f32[128,80,128]{2,1,0:T(8,128)}, u32[]{:S(2)}, u32[]{:S(2)}) %all-to-all-start.3) | async-done | bytes 5242912 | tf_op jit(solution)/shard_map/all_to_all | solution.py:545
  235.2 2.3 slice.4
  237.5 1.3 collective-permute-start.1
  238.8 3.6 %all-to-all-start.4 = ((f32[128,32,128]{2,1,0:T(8,128)}), f32[128,32,128]{2,1,0:T(8,128)S(1)}, u32[]{:S(2)}, u32[]{:S(2)}) async-start(f32[128,32,128]{2,1,0:T(8,128)} %bitcast.16), calls=%async_computation.4 | async-start | bytes 4194304 | tf_op jit(solution)/shard_map/all_to_all | solution.py:545
  242.4 0.0 collective-permute-done.1.other_ref
  242.4 6.9 %panel.1.part_ref = f32[512,1024]{1,0:T(8,128)} custom-call(s32[2]{0:T(128)} %pad_add_fusion.where_ref, f32[10240,128]{1,0:T(8,128)} %bitcast.13.in_ref, f32[2048,128]{1,0:T(8,128)} %collective-permute-done.1.other_ref, f32[1024,1024]{1,0:T(8,128)} %get-tuple-element.35.l_ref, f32[1024,256]{1,0:T(8,128)} %get-tuple-element.36.inv_ref), custom_call_target="tpu_custom_call" | custom-call | flops 20000000000 | bytes 20000000 | tf_op jit(solution)/shard_map/panel/pallas_call | solution.py:485
  249.4 23.6 %all-to-all-done.4 = f32[128,32,128]{2,1,0:T(8,128)S(1)} async-done(((f32[128,32,128]{2,1,0:T(8,128)}), f32[128,32,128]{2,1,0:T(8,128)S(1)}, u32[]{:S(2)}, u32[]{:S(2)}) %all-to-all-start.4) | async-done | bytes 2097184 | tf_op jit(solution)/shard_map/all_to_all | solution.py:545
  273.0 0.0 copy-start
  273.0 1.3 copy-done
  274.3 3.7 %finish.1 = f32[512,1024]{1,0:T(8,128)} custom-call(s32[2]{0:T(128)} %pad_add_fusion.where_ref, f32[512,1024]{1,0:T(8,128)} %panel.1.part_ref, f32[4096,128]{1,0:T(8,128)} %bitcast.32), custom_call_target="tpu_custom_call" | custom-call | flops 6000000000 | bytes 6000000 | tf_op jit(solution)/shard_map/finish/pallas_call | solution.py:532
Async XLA Ops:
  4.3 42.0 %all-to-all-start = ((f32[128,32,128]{2,1,0:T(8,128)}), f32[128,32,128]{2,1,0:T(8,128)S(1)}, u32[]{:S(2)}, u32[]{:S(2)}) async-start(f32[128,32,128]{2,1,0:T(8,128)} %copy_bitcast_fusion), calls=%async_computation | async-start | bytes 4194304 | tf_op jit(solution)/shard_map/all_to_all | solution.py:545
  46.3 72.2 %copy-start.1 = (f32[128,32,128]{2,1,0:T(8,128)}, f32[128,32,128]{2,1,0:T(8,128)S(1)}, u32[]{:S(2)}) copy-start(f32[128,32,128]{2,1,0:T(8,128)S(1)} %all-to-all-done) | copy-start | bytes 6291460
  135.3 29.4 %all-to-all-start.2 = ((f32[128,24,128]{2,1,0:T(8,128)}), f32[128,24,128]{2,1,0:T(8,128)S(1)}, u32[]{:S(2)}, u32[]{:S(2)}) async-start(f32[128,24,128]{2,1,0:T(8,128)} %bitcast.36), calls=%async_computation.2 | async-start | bytes 3145728 | tf_op jit(solution)/shard_map/all_to_all | solution.py:545
  164.7 1.2 copy-start.2
  164.7 7.2 %collective-permute-start = (f32[3072,128]{1,0:T(8,128)S(1)}, f32[3072,128]{1,0:T(8,128)}, u32[]{:S(2)}, u32[]{:S(2)}) collective-permute-start(f32[3072,128]{1,0:T(8,128)S(1)} %bitcast.34), channel_id=1, source_target_pairs={{0,1},{1,0},{2,3},{3,2},{4,5},{5,4},{6,7},{7,6},{8,9},{9,8},{10,11... | collective-permute-start | bytes 4718600 | tf_op jit(solution)/shard_map/ppermute | solution.py:549
  165.9 69.3 %all-to-all-start.3 = ((f32[128,80,128]{2,1,0:T(8,128)}), f32[128,80,128]{2,1,0:T(8,128)}, u32[]{:S(2)}, u32[]{:S(2)}) async-start(f32[128,80,128]{2,1,0:T(8,128)} %bitcast.29), calls=%async_computation.3 | async-start | bytes 10485760 | tf_op jit(solution)/shard_map/all_to_all | solution.py:545
  237.5 4.9 %collective-permute-start.1 = (f32[2048,128]{1,0:T(8,128)}, f32[2048,128]{1,0:T(8,128)}, u32[]{:S(2)}, u32[]{:S(2)}) collective-permute-start(f32[2048,128]{1,0:T(8,128)} %bitcast.15), channel_id=1, source_target_pairs={{0,1},{1,0},{2,3},{3,2},{4,5},{5,4},{6,7},{7,6},{8,9},{9,8},{10,11... | collective-permute-start | bytes 3145736 | tf_op jit(solution)/shard_map/ppermute | solution.py:549
  238.8 34.1 %all-to-all-start.4 = ((f32[128,32,128]{2,1,0:T(8,128)}), f32[128,32,128]{2,1,0:T(8,128)S(1)}, u32[]{:S(2)}, u32[]{:S(2)}) async-start(f32[128,32,128]{2,1,0:T(8,128)} %bitcast.16), calls=%async_computation.4 | async-start | bytes 4194304 | tf_op jit(solution)/shard_map/all_to_all | solution.py:545
  273.0 1.3 copy-start
